TPU v7x, 128 devices: a whole 4x4x4 slice. The times are simulated.
128 devices in a mesh: dp: 8 (over y, core), fsdp: 16 (over z, x).
Axes of the slice: x: 4, y: 4, z: 4, core: 2. Of those that a mesh axis runs over, the one named last changes fastest.
Arguments:
- tokens: bfloat16 [16384, 1024], P(('dp', 'fsdp')), may hold values from -20 to 20, as said below
- segment: int32 [128, 128], P(('dp', 'fsdp')), may hold values from 0 to 1, as said below
- norm_gain: float32 [1024], P(('dp', 'fsdp')), may hold values from 0.5 to 1.5
- w_query: float32 [1024, 2048], P(('dp', 'fsdp')), may hold values from -0.1875 to 0.1875
- w_key: float32 [1024, 1024], P(('dp', 'fsdp')), may hold values from -0.1875 to 0.1875
- w_value: float32 [1024, 1024], P(('dp', 'fsdp')), may hold values from -0.1875 to 0.1875
- query_gain: float32 [128], P(('dp', 'fsdp')), may hold values from 0.1 to 1.9
- key_gain: float32 [128], P(('dp', 'fsdp')), may hold values from 0.1 to 1.9
- w_out: float32 [2048, 1024], P(('dp', 'fsdp')), may hold values from -0.75 to 0.75
- mlp_gain: float32 [1024], P(('dp', 'fsdp')), may hold values from 0.5 to 1.5
- w_gate: float32 [1024, 3072], P(('dp', 'fsdp')), may hold values from -0.1875 to 0.1875
- w_up: float32 [1024, 3072], P(('dp', 'fsdp')), may hold values from -0.1875 to 0.1875
- w_down: float32 [3072, 1024], P(('dp', 'fsdp')), may hold values from -0.21875 to 0.21875
- cotangent: bfloat16 [16384, 1024], P(('dp', 'fsdp')), may hold values from -6 to 6
Outputs:
- layer_out: bfloat16 [16384, 1024], P(('dp', 'fsdp'))
- input_grad: float32 [16384, 1024], P(('dp', 'fsdp'))
- grad_norm_gain: float32 [1024], P(('dp', 'fsdp'))
- grad_w_query: float32 [1024, 2048], P(('dp', 'fsdp'))
- grad_w_key: float32 [1024, 1024], P(('dp', 'fsdp'))
- grad_w_value: float32 [1024, 1024], P(('dp', 'fsdp'))
- grad_query_gain: float32 [128], P(('dp', 'fsdp'))
- grad_key_gain: float32 [128], P(('dp', 'fsdp'))
- grad_w_out: float32 [2048, 1024], P(('dp', 'fsdp'))
- grad_mlp_gain: float32 [1024], P(('dp', 'fsdp'))
- grad_w_gate: float32 [1024, 3072], P(('dp', 'fsdp'))
- grad_w_up: float32 [1024, 3072], P(('dp', 'fsdp'))
- grad_w_down: float32 [3072, 1024], P(('dp', 'fsdp'))
Inputs may be any that keep to these rules, and one draw needn't show every extreme that they name: `segment`: in each row (one device's tokens) the ids never fall; a row holds one or two sequences, each of 48 to 128 tokens, and some row holds one sequence of exactly 128. `tokens`: rows have different scales.
All inputs are finite; a program needn't handle non-finite values.
Results may differ from a plain program's by a relative error of at most 0.033.
Values may be sent and summed in bfloat16 or wider, within the bound.
A program may use at most 192 MiB of HBM per device.

v0:
```python
import jax
import jax.numpy as jnp
from jax import lax
from jax.sharding import PartitionSpec as P

HQ = 16
HK = 8
HD = 128


EPS = 1e-06
THETA = 1000000.0


def contract(left, right, left_dim, right_dim):
    return lax.dot_general(
        left, right, (((left_dim,), (right_dim,)), ((), ())), preferred_element_type=jnp.float32
    )


def inverse_rms(vector):
    return lax.rsqrt(jnp.mean(vector * vector, axis=-1, keepdims=True) + EPS)


def norm_backward(grad_in, unit_vec, inverse, gain_vec):
    scaled = grad_in * gain_vec
    return inverse * (scaled - unit_vec * jnp.mean(scaled * unit_vec, axis=-1, keepdims=True))


def rotate(vector, cos_part, sin_part):
    half_dim = vector.shape[-1] // 2
    first_half = vector[..., :half_dim]
    second_half = vector[..., half_dim:]
    return jnp.concatenate(
        [
            first_half * cos_part - second_half * sin_part,
            second_half * cos_part + first_half * sin_part,
        ],
        axis=-1,
    )


def unrotate(vector, cos_part, sin_part):
    half_dim = vector.shape[-1] // 2
    first_half = vector[..., :half_dim]
    second_half = vector[..., half_dim:]
    return jnp.concatenate(
        [
            first_half * cos_part + second_half * sin_part,
            second_half * cos_part - first_half * sin_part,
        ],
        axis=-1,
    )


def body(
    tokens,
    segment,
    norm_gain,
    w_query,
    w_key,
    w_value,
    query_gain,
    key_gain,
    w_out,
    mlp_gain,
    w_gate,
    w_up,
    w_down,
    cotangent,
):
    bf16 = jnp.bfloat16
    f32 = jnp.float32
    low_attn = [
        weight.astype(bf16)
        for weight in (norm_gain, w_query, w_key, w_value, query_gain, key_gain, w_out)
    ]
    low_mlp = [weight.astype(bf16) for weight in (mlp_gain, w_gate, w_up, w_down)]
    attn_set = (
        lax.all_gather(low_attn[0], ("dp", "fsdp"), axis=0, tiled=True),
        lax.all_gather(low_attn[1], ("dp", "fsdp"), axis=0, tiled=True),
        lax.all_gather(low_attn[2], ("dp", "fsdp"), axis=0, tiled=True),
        lax.all_gather(low_attn[3], ("dp", "fsdp"), axis=0, tiled=True),
        lax.all_gather(low_attn[4], ("dp", "fsdp"), axis=0, tiled=True),
        lax.all_gather(low_attn[5], ("dp", "fsdp"), axis=0, tiled=True),
        lax.all_gather(low_attn[6], ("dp", "fsdp"), axis=0, tiled=True),
    )
    row_count = tokens.shape[0]
    seg_ids = segment[0]
    row_index = jnp.arange(row_count, dtype=jnp.int32)
    same_seq = seg_ids[:, None] == seg_ids[None, :]
    allowed = same_seq & (row_index[None, :] <= row_index[:, None])
    position = jnp.sum(
        (same_seq & (row_index[None, :] < row_index[:, None])).astype(jnp.int32), axis=1
    )
    half_dim = HD // 2
    inv_freq = THETA ** (-jnp.arange(half_dim, dtype=f32) * 2.0 / HD)
    angles = position.astype(f32)[:, None] * inv_freq[None, :]
    cos_part = jnp.cos(angles)[:, None, :]
    sin_part = jnp.sin(angles)[:, None, :]
    group_size = HQ // HK
    score_scale = HD ** (-0.5)
    gain_in = attn_set[0].astype(f32)
    gain_query = attn_set[4].astype(f32)
    gain_key = attn_set[5].astype(f32)
    x_float = tokens.astype(f32)
    inv_in = inverse_rms(x_float)
    unit_in = x_float * inv_in
    normed = (unit_in * gain_in).astype(bf16)
    q_raw = jnp.dot(normed, attn_set[1], preferred_element_type=f32).reshape(row_count, HQ, HD)
    k_raw = jnp.dot(normed, attn_set[2], preferred_element_type=f32).reshape(row_count, HK, HD)
    values_low = (
        jnp.dot(normed, attn_set[3], preferred_element_type=f32)
        .astype(bf16)
        .reshape(row_count, HK, HD)
    )
    inv_q = inverse_rms(q_raw)
    unit_q = q_raw * inv_q
    inv_k = inverse_rms(k_raw)
    unit_k = k_raw * inv_k
    q_rot = rotate(unit_q * gain_query, cos_part, sin_part).astype(bf16)
    k_rot = rotate(unit_k * gain_key, cos_part, sin_part).astype(bf16)
    q_group = q_rot.reshape(row_count, HK, group_size, HD)
    scores = jnp.einsum("qhgd,khd->hgqk", q_group, k_rot, preferred_element_type=f32) * score_scale
    masked = jnp.where(allowed[None, None], scores, -1e30)
    exp_terms = jnp.exp(masked - jnp.max(masked, axis=-1, keepdims=True))
    prob_full = exp_terms / jnp.sum(exp_terms, axis=-1, keepdims=True)
    prob_low = prob_full.astype(bf16)
    attended = (
        jnp.einsum("hgqk,khd->qhgd", prob_low, values_low, preferred_element_type=f32)
        .reshape(row_count, HQ * HD)
        .astype(bf16)
    )
    hidden_res = x_float + jnp.dot(attended, attn_set[6], preferred_element_type=f32)
    mlp_set = (
        lax.all_gather(low_mlp[0], ("dp", "fsdp"), axis=0, tiled=True),
        lax.all_gather(low_mlp[1], ("dp", "fsdp"), axis=0, tiled=True),
        lax.all_gather(low_mlp[2], ("dp", "fsdp"), axis=0, tiled=True),
        lax.all_gather(low_mlp[3], ("dp", "fsdp"), axis=0, tiled=True),
    )
    gain_mid = mlp_set[0].astype(f32)
    inv_mid = inverse_rms(hidden_res)
    unit_mid = hidden_res * inv_mid
    mid_low = (unit_mid * gain_mid).astype(bf16)
    gate_proj = jnp.dot(mid_low, mlp_set[1], preferred_element_type=f32)
    up_proj = jnp.dot(mid_low, mlp_set[2], preferred_element_type=f32)
    sig_gate = jax.nn.sigmoid(gate_proj)
    act_gate = gate_proj * sig_gate
    mixed = (act_gate * up_proj).astype(bf16)
    layer_sum = hidden_res + jnp.dot(mixed, mlp_set[3], preferred_element_type=f32)
    layer_out = layer_sum.astype(bf16)
    mlp_back = (
        lax.all_gather(low_mlp[0], ("dp", "fsdp"), axis=0, tiled=True),
        lax.all_gather(low_mlp[1], ("dp", "fsdp"), axis=0, tiled=True),
        lax.all_gather(low_mlp[2], ("dp", "fsdp"), axis=0, tiled=True),
        lax.all_gather(low_mlp[3], ("dp", "fsdp"), axis=0, tiled=True),
    )
    cot_float = cotangent.astype(f32)
    grad_w_down = contract(mixed, cotangent, 0, 0)
    d_mixed = contract(cotangent, mlp_back[3], 1, 1)
    d_gate = (d_mixed * up_proj * sig_gate * (1.0 + gate_proj * (1.0 - sig_gate))).astype(bf16)
    d_up = (d_mixed * act_gate).astype(bf16)
    grad_w_gate = contract(mid_low, d_gate, 0, 0)
    grad_w_up = contract(mid_low, d_up, 0, 0)
    d_mid = contract(d_gate, mlp_back[1], 1, 1) + contract(d_up, mlp_back[2], 1, 1)
    grad_mlp_gain = jnp.sum(d_mid * unit_mid, axis=0)
    d_res = cot_float + norm_backward(d_mid, unit_mid, inv_mid, mlp_back[0].astype(f32))
    attn_back = (
        lax.all_gather(low_attn[0], ("dp", "fsdp"), axis=0, tiled=True),
        lax.all_gather(low_attn[1], ("dp", "fsdp"), axis=0, tiled=True),
        lax.all_gather(low_attn[2], ("dp", "fsdp"), axis=0, tiled=True),
        lax.all_gather(low_attn[3], ("dp", "fsdp"), axis=0, tiled=True),
        lax.all_gather(low_attn[4], ("dp", "fsdp"), axis=0, tiled=True),
        lax.all_gather(low_attn[5], ("dp", "fsdp"), axis=0, tiled=True),
        lax.all_gather(low_attn[6], ("dp", "fsdp"), axis=0, tiled=True),
    )
    d_res_low = d_res.astype(bf16)
    grad_w_out = contract(attended, d_res_low, 0, 0)
    d_attn = (
        contract(d_res_low, attn_back[6], 1, 1).astype(bf16).reshape(row_count, HK, group_size, HD)
    )
    d_probs = jnp.einsum("qhgd,khd->hgqk", d_attn, values_low, preferred_element_type=f32)
    d_values = (
        jnp.einsum("hgqk,qhgd->khd", prob_low, d_attn, preferred_element_type=f32)
        .astype(bf16)
        .reshape(row_count, HK * HD)
    )
    d_scores = (
        prob_full * (d_probs - jnp.sum(d_probs * prob_full, axis=-1, keepdims=True))
    ).astype(bf16)
    d_qrot = (
        jnp.einsum("hgqk,khd->qhgd", d_scores, k_rot, preferred_element_type=f32) * score_scale
    ).reshape(row_count, HQ, HD)
    d_krot = (
        jnp.einsum("hgqk,qhgd->khd", d_scores, q_group, preferred_element_type=f32) * score_scale
    )
    d_qunit = unrotate(d_qrot, cos_part, sin_part)
    d_kunit = unrotate(d_krot, cos_part, sin_part)
    grad_query_gain = jnp.sum(d_qunit * unit_q, axis=(0, 1))
    grad_key_gain = jnp.sum(d_kunit * unit_k, axis=(0, 1))
    d_qraw = (
        norm_backward(d_qunit, unit_q, inv_q, attn_back[4].astype(f32))
        .astype(bf16)
        .reshape(row_count, HQ * HD)
    )
    d_kraw = (
        norm_backward(d_kunit, unit_k, inv_k, attn_back[5].astype(f32))
        .astype(bf16)
        .reshape(row_count, HK * HD)
    )
    grad_w_query = contract(normed, d_qraw, 0, 0)
    grad_w_key = contract(normed, d_kraw, 0, 0)
    grad_w_value = contract(normed, d_values, 0, 0)
    d_normed = (
        contract(d_qraw, attn_back[1], 1, 1)
        + contract(d_kraw, attn_back[2], 1, 1)
        + contract(d_values, attn_back[3], 1, 1)
    )
    grad_norm_gain = jnp.sum(d_normed * unit_in, axis=0)
    input_grad = d_res + norm_backward(d_normed, unit_in, inv_in, attn_back[0].astype(f32))
    summed = tuple(
        (
            lax.psum_scatter(grad_norm_gain, ("dp", "fsdp"), scatter_dimension=0, tiled=True),
            lax.psum_scatter(grad_w_query, ("dp", "fsdp"), scatter_dimension=0, tiled=True),
            lax.psum_scatter(grad_w_key, ("dp", "fsdp"), scatter_dimension=0, tiled=True),
            lax.psum_scatter(grad_w_value, ("dp", "fsdp"), scatter_dimension=0, tiled=True),
            lax.psum_scatter(grad_query_gain, ("dp", "fsdp"), scatter_dimension=0, tiled=True),
            lax.psum_scatter(grad_key_gain, ("dp", "fsdp"), scatter_dimension=0, tiled=True),
            lax.psum_scatter(grad_w_out, ("dp", "fsdp"), scatter_dimension=0, tiled=True),
            lax.psum_scatter(grad_mlp_gain, ("dp", "fsdp"), scatter_dimension=0, tiled=True),
            lax.psum_scatter(grad_w_gate, ("dp", "fsdp"), scatter_dimension=0, tiled=True),
            lax.psum_scatter(grad_w_up, ("dp", "fsdp"), scatter_dimension=0, tiled=True),
            lax.psum_scatter(grad_w_down, ("dp", "fsdp"), scatter_dimension=0, tiled=True),
        )
    )
    return (
        layer_out,
        input_grad,
        summed[0],
        summed[1],
        summed[2],
        summed[3],
        summed[4],
        summed[5],
        summed[6],
        summed[7],
        summed[8],
        summed[9],
        summed[10],
    )


def solution(mesh):
    return jax.shard_map(
        body,
        mesh=mesh,
        in_specs=(
            P(("dp", "fsdp"), None),
            P(("dp", "fsdp"), None),
            P(("dp", "fsdp")),
            P(("dp", "fsdp"), None),
            P(("dp", "fsdp"), None),
            P(("dp", "fsdp"), None),
            P(("dp", "fsdp")),
            P(("dp", "fsdp")),
            P(("dp", "fsdp"), None),
            P(("dp", "fsdp")),
            P(("dp", "fsdp"), None),
            P(("dp", "fsdp"), None),
            P(("dp", "fsdp"), None),
            P(("dp", "fsdp"), None),
        ),
        out_specs=(
            P(("dp", "fsdp"), None),
            P(("dp", "fsdp"), None),
            P(("dp", "fsdp")),
            P(("dp", "fsdp"), None),
            P(("dp", "fsdp"), None),
            P(("dp", "fsdp"), None),
            P(("dp", "fsdp")),
            P(("dp", "fsdp")),
            P(("dp", "fsdp"), None),
            P(("dp", "fsdp")),
            P(("dp", "fsdp"), None),
            P(("dp", "fsdp"), None),
            P(("dp", "fsdp"), None),
        ),
        check_vma=False,
    )
```

profile of v0, /device:TPU:1, one launch (start us, length us, event | category | flops | bytes accessed | tf_op | source)
XLA Modules:
  0.0 3784.2 jit_solution(12498452885531330073)
XLA Ops:
  14.8 1.5 convert_element_type.147
  21.3 69.8 %all-reduce.9 = (bf16[1024]{0:T(1024)(128)(2,1)S(1)}, bf16[128]{0:T(256)(128)(2,1)S(1)}, bf16[128]{0:T(256)(128)(2,1)S(1)}, bf16[1024]{0:T(1024)(128)(2,1)S(1)}) all-reduce(bf16[1024]{0:T(1024)(128)(2,1)S(1)} %dynamic-update-slice, bf16[128]{0:T(256)(128)(2,1)S(1)} %dynamic-update-slice.2, ...), channel_id=1, replica_groups=mesh['dp'=8,'fsdp'=16] {'dp','fsdp'}, use_global_device_ids=true, to_apply=%add | all-reduce | flops 2304 | bytes 9216
  95.5 2.2 fusion.55
  98.0 48.7 %all-gather.8.cloned.1.call-done = bf16[1024,1024]{1,0:T(8,128)(2,1)} async-done(((bf16[8,1024]{1,0:T(8,128)(2,1)}), bf16[1024,1024]{1,0:T(8,128)(2,1)}) %all-gather.8.cloned.1.call-update) | async-done | bytes 2097168 | tf_op jit(solution)/shard_map/all_gather | solution.py:83
  146.8 2.1 fusion.11
  150.9 64.0 %all-gather.12.cloned.1.call-done = bf16[1024,2048]{1,0:T(8,128)(2,1)} async-done(((bf16[8,2048]{1,0:T(8,128)(2,1)}), bf16[1024,2048]{1,0:T(8,128)(2,1)}) %all-gather.12.cloned.1.call-update) | async-done | bytes 4194320 | tf_op jit(solution)/shard_map/all_gather | solution.py:81
  214.9 3.0 fusion.53
  220.7 3.1 fusion.59
  223.8 2.0 convolution_convert_fusion.1
  225.8 57.0 %all-gather.14.cloned.1.call-done = bf16[2048,1024]{1,0:T(8,128)(2,1)} async-done(((bf16[16,1024]{1,0:T(8,128)(2,1)}), bf16[2048,1024]{1,0:T(8,128)(2,1)}) %all-gather.14.cloned.1.call-update) | async-done | bytes 4194320 | tf_op jit(solution)/shard_map/all_gather | solution.py:86
  282.8 3.0 multiply_reduce_fusion.6
  285.9 66.0 %all-gather.16.cloned.1.call-done = bf16[1024,3072]{1,0:T(8,128)(2,1)} async-done(((bf16[8,3072]{1,0:T(8,128)(2,1)}), bf16[1024,3072]{1,0:T(8,128)(2,1)}) %all-gather.16.cloned.1.call-update) | async-done | bytes 6291472 | tf_op jit(solution)/shard_map/all_gather | solution.py:137
  351.9 4.9 fusion.60
  356.9 64.4 %all-gather.18.cloned.1.call-done = bf16[1024,3072]{1,0:T(8,128)(2,1)} async-done(((bf16[8,3072]{1,0:T(8,128)(2,1)}), bf16[1024,3072]{1,0:T(8,128)(2,1)}) %all-gather.18.cloned.1.call-update) | async-done | bytes 6291472 | tf_op jit(solution)/shard_map/all_gather | solution.py:138
  421.3 4.9 fusion.61
  426.2 64.6 %all-gather.20.cloned.1.call-done = bf16[3072,1024]{1,0:T(8,128)(2,1)} async-done(((bf16[24,1024]{1,0:T(8,128)(2,1)}), bf16[3072,1024]{1,0:T(8,128)(2,1)}) %all-gather.20.cloned.1.call-update) | async-done | bytes 6291472 | tf_op jit(solution)/shard_map/all_gather | solution.py:139
  490.8 7.1 multiply_convert_fusion
  497.9 5.8 fusion.62
  503.7 2.9 multiply_reduce_fusion.3
  507.5 2.3 convolution_convert_fusion
  509.8 2.0 copy.148
  511.8 1.9 multiply_reduce_fusion.1
  517.2 1.9 fusion.30
  519.2 2.8 fusion.49
  522.0 3.0 fusion.10
  525.0 3.9 fusion.47
  529.8 1.5 convolution_multiply_fusion
  532.2 2.4 copy.145
  536.0 1.8 multiply_add_fusion
  539.5 1.6 fusion.15
  541.1 4.5 fusion.51
  546.8 6.3 fusion.65
  554.3 6.3 fusion.66
  561.6 4.5 fusion.37
  567.4 6.4 fusion.67
  574.5 2.8 fusion.63
  577.3 2.4 fusion.64
  579.8 2.4 fusion.25
  582.2 63.9 %all-reduce.8 = (f32[1024]{0:T(1024)S(1)}, f32[128]{0:T(128)S(1)}, f32[128]{0:T(128)S(1)}, f32[1024]{0:T(1024)S(1)}) all-reduce(f32[1024]{0:T(1024)S(1)} %get-tuple-element.15, f32[128]{0:T(128)S(1)} %bitcast_reduce_fusion, f32[128]{0:T(128)S(1)} %bitcast_reduce_fusion.1, ...), channel_id=2, replica_groups=mesh['dp'=8,'fsdp'=16] {'dp','fsdp'}, use_global_device_ids=true, to_apply=%region_13.14.clone | all-reduce | flops 2304 | bytes 18432
  648.4 2.1 fusion.24
  650.4 4.5 fusion.9
  654.9 476.6 %reduce-scatter.10.cloned.1.call-done = f32[8,1024]{1,0:T(8,128)} async-done(((f32[1024,1024]{1,0:T(8,128)}), f32[8,1024]{1,0:T(8,128)}) %reduce-scatter.10.cloned.1.call-update) | async-done | bytes 32784 | tf_op jit(solution)/shard_map/reduce_scatter | solution.py:225
  1131.5 641.1 %reduce-scatter.12.cloned.1.call-done = f32[8,1024]{1,0:T(8,128)} async-done(((f32[1024,1024]{1,0:T(8,128)}), f32[8,1024]{1,0:T(8,128)}) %reduce-scatter.12.cloned.1.call-update) | async-done | bytes 32784 | tf_op jit(solution)/shard_map/reduce_scatter | solution.py:226
  1772.6 651.0 %reduce-scatter.8.cloned.1.call-done = f32[8,2048]{1,0:T(8,128)} async-done(((f32[1024,2048]{1,0:T(8,128)}), f32[8,2048]{1,0:T(8,128)}) %reduce-scatter.8.cloned.1.call-update) | async-done | bytes 65552 | tf_op jit(solution)/shard_map/reduce_scatter | solution.py:224
  2423.6 252.0 %reduce-scatter.16.cloned.1.call-done = f32[8,3072]{1,0:T(8,128)} async-done(((f32[1024,3072]{1,0:T(8,128)}), f32[8,3072]{1,0:T(8,128)}) %reduce-scatter.16.cloned.1.call-update) | async-done | bytes 98320 | tf_op jit(solution)/shard_map/reduce_scatter | solution.py:231
  2675.7 225.4 %reduce-scatter.18.cloned.1.call-done = f32[8,3072]{1,0:T(8,128)} async-done(((f32[1024,3072]{1,0:T(8,128)}), f32[8,3072]{1,0:T(8,128)}) %reduce-scatter.18.cloned.1.call-update) | async-done | bytes 98320 | tf_op jit(solution)/shard_map/reduce_scatter | solution.py:232
  2901.1 625.2 %reduce-scatter.14.cloned.1.call-done = f32[16,1024]{1,0:T(8,128)} async-done(((f32[2048,1024]{1,0:T(8,128)}), f32[16,1024]{1,0:T(8,128)}) %reduce-scatter.14.cloned.1.call-update) | async-done | bytes 65552 | tf_op jit(solution)/shard_map/reduce_scatter | solution.py:229
  3526.3 251.1 %reduce-scatter.20.cloned.1.call-done = f32[24,1024]{1,0:T(8,128)} async-done(((f32[3072,1024]{1,0:T(8,128)}), f32[24,1024]{1,0:T(8,128)}) %reduce-scatter.20.cloned.1.call-update) | async-done | bytes 98320 | tf_op jit(solution)/shard_map/reduce_scatter | solution.py:233
  (178 shorter events, 37.3 us)
Async XLA Ops:
  7.2 139.6 %copy-start.1 = (bf16[128,1024]{1,0:T(8,128)(2,1)S(1)}, bf16[128,1024]{1,0:T(8,128)(2,1)}, u32[]{:S(2)}) copy-start(bf16[128,1024]{1,0:T(8,128)(2,1)} %param.14) | copy-start | bytes 786436
  7.2 88.3 %all-gather.10.cloned.1.call-start = ((), (), s32[]{:S(2)}) async-start(), calls=%async_computation.8 | async-start | bytes 2113536 | tf_op jit(solution)/shard_map/all_gather | solution.py:82
  8.7 138.1 %all-gather.8.cloned.1.call-start = ((), (), s32[]{:S(2)}) async-start(), calls=%async_computation.7 | async-start | bytes 2113536 | tf_op jit(solution)/shard_map/all_gather | solution.py:83
  10.1 204.8 %all-gather.12.cloned.1.call-start = ((), (), s32[]{:S(2)}) async-start(), calls=%async_computation.9 | async-start | bytes 4227072 | tf_op jit(solution)/shard_map/all_gather | solution.py:81
  11.6 271.2 %all-gather.14.cloned.1.call-start = ((), (), s32[]{:S(2)}) async-start(), calls=%async_computation.10 | async-start | bytes 4227072 | tf_op jit(solution)/shard_map/all_gather | solution.py:86
  13.2 338.8 %all-gather.16.cloned.1.call-start = ((), (), s32[]{:S(2)}) async-start(), calls=%async_computation.11 | async-start | bytes 6340608 | tf_op jit(solution)/shard_map/all_gather | solution.py:137
  14.8 406.5 %all-gather.18.cloned.1.call-start = ((), (), s32[]{:S(2)}) async-start(), calls=%async_computation.12 | async-start | bytes 6340608 | tf_op jit(solution)/shard_map/all_gather | solution.py:138
  16.4 474.5 %all-gather.20.cloned.1.call-start = ((), (), s32[]{:S(2)}) async-start(), calls=%async_computation.13 | async-start | bytes 6340608 | tf_op jit(solution)/shard_map/all_gather | solution.py:139
  18.0 1113.6 %reduce-scatter.10.cloned.1.call-start = ((), (), s32[]{:S(2)}) async-start(), calls=%async_computation.15 | async-start | bytes 4227072 | tf_op jit(solution)/shard_map/reduce_scatter | solution.py:225
  91.1 59.4 %copy-start.37 = (f32[128]{0:T(128)}, f32[128]{0:T(128)S(1)}, u32[]{:S(2)}) copy-start(f32[128]{0:T(128)S(1)} %convert_element_type.132) | copy-start | bytes 1540
  92.0 126.8 %copy-start.35 = (f32[128]{0:T(128)}, f32[128]{0:T(128)S(1)}, u32[]{:S(2)}) copy-start(f32[128]{0:T(128)S(1)} %convert_element_type.137) | copy-start | bytes 1540
  150.9 69.8 %copy-start.26 = (bf16[128,8,64]{2,0,1:T(8,128)(2,1)}, bf16[128,8,64]{2,0,1:T(8,128)(2,1)S(1)}, u32[]{:S(2)}) copy-start(bf16[128,8,64]{2,0,1:T(8,128)(2,1)S(1)} %get-tuple-element.44) | copy-start | bytes 393220
  150.9 69.8 %copy-start.27 = (bf16[128,8,64]{2,0,1:T(8,128)(2,1)}, bf16[128,8,64]{2,0,1:T(8,128)(2,1)S(1)}, u32[]{:S(2)}) copy-start(bf16[128,8,64]{2,0,1:T(8,128)(2,1)S(1)} %get-tuple-element.45) | copy-start | bytes 393220
  220.5 5.3 copy-start.15
  220.7 5.2 copy-start.18
  225.8 60.0 %copy-start.9 = (bf16[8,128,2,128]{3,1,2,0:T(8,128)(2,1)}, bf16[8,128,2,128]{3,1,2,0:T(8,128)(2,1)S(1)}, u32[]{:S(2)}) copy-start(bf16[8,128,2,128]{3,1,2,0:T(8,128)(2,1)S(1)} %convolution_convert_fusion.1) | copy-start | bytes 1572868
  285.8 217.9 %copy-start.39 = (f32[128]{0:T(128)}, f32[128]{0:T(128)S(1)}, u32[]{:S(2)}) copy-start(f32[128]{0:T(128)S(1)} %add_rsqrt_fusion.2) | copy-start | bytes 1540
  356.9 133.9 %copy-start.20 = (bf16[128,1024]{1,0:T(8,128)(2,1)S(1)}, bf16[128,1024]{1,0:T(8,128)(2,1)}, u32[]{:S(2)}) copy-start(bf16[128,1024]{1,0:T(8,128)(2,1)} %param.27) | copy-start | bytes 786436
  497.9 8.7 copy-start.11
  497.9 8.7 copy-start.13
  497.9 5.8 copy-start
  503.7 3.8 copy-start.2
  507.5 6.3 copy-start.33
  511.8 1.9 copy-start.24
  511.8 3.0 copy-start.16
  511.8 3.0 copy-start.19
  513.8 1.8 copy-start.38
  514.8 2.2 copy-start.28
  514.8 2.4 copy-start.32
  519.2 2.8 copy-start.17
  519.2 2.9 copy-start.34
  522.0 1250.7 %reduce-scatter.12.cloned.1.call-start = ((), (), s32[]{:S(2)}) async-start(), calls=%async_computation.16 | async-start | bytes 4227072 | tf_op jit(solution)/shard_map/reduce_scatter | solution.py:226
  525.0 4.2 copy-start.36
  525.0 4.8 copy-start.7
  528.9 1894.7 %reduce-scatter.8.cloned.1.call-start = ((), (), s32[]{:S(2)}) async-start(), calls=%async_computation.14 | async-start | bytes 8454144 | tf_op jit(solution)/shard_map/reduce_scatter | solution.py:224
  536.0 1.8 copy-start.23
  537.8 1.7 copy-start.5
  537.8 1.7 copy-start.29
  545.7 1.1 copy-start.12
  545.7 2130.0 %reduce-scatter.16.cloned.1.call-start = ((), (), s32[]{:S(2)}) async-start(), calls=%async_computation.18 | async-start | bytes 12681216 | tf_op jit(solution)/shard_map/reduce_scatter | solution.py:231
  553.1 1.1 copy-start.14
  553.2 2347.9 %reduce-scatter.18.cloned.1.call-start = ((), (), s32[]{:S(2)}) async-start(), calls=%async_computation.19 | async-start | bytes 12681216 | tf_op jit(solution)/shard_map/reduce_scatter | solution.py:232
  560.6 2965.7 %reduce-scatter.14.cloned.1.call-start = ((), (), s32[]{:S(2)}) async-start(), calls=%async_computation.17 | async-start | bytes 8454144 | tf_op jit(solution)/shard_map/reduce_scatter | solution.py:229
  566.2 1.2 copy-start.21
  566.2 3211.2 %reduce-scatter.20.cloned.1.call-start = ((), (), s32[]{:S(2)}) async-start(), calls=%async_computation.20 | async-start | bytes 12681216 | tf_op jit(solution)/shard_map/reduce_scatter | solution.py:233
  573.8 3.5 copy-start.25
  573.8 5.9 copy-start.3
  577.3 4.9 copy-start.30
  (6 other events, 5.3 us)
Sparse Core Ops, SparseCore 0:
  11.6 68.8 all-gather.9
  84.0 62.7 all-gather.7
  150.5 64.2 all-gather.11
  218.4 64.3 all-gather.13
  286.3 65.5 all-gather.15
  355.5 65.8 all-gather.17
  425.0 65.8 all-gather.19
  522.1 609.4 reduce-scatter.9
  1134.6 638.0 reduce-scatter.11
  1775.4 648.1 reduce-scatter.7
  2430.0 245.6 reduce-scatter.15
  2681.9 219.1 reduce-scatter.17
  2904.1 622.0 reduce-scatter.13
  3531.7 245.6 reduce-scatter.19
where the time goes:
time: 3790 us; the launch traced here: 3780 us
  waiting for transfers between devices  3490 us (92%)
  blocking collectives  134 us (4%)
  matrix products  97 us (3%)
    reduce_scatter x1, waiting for transfers between devices, body(): lax.psum_scatter(grad_w_query, ('dp', 'fsdp'), scatter_dimension=0, tiled...  651 us
    reduce_scatter x1, waiting for transfers between devices, body(): lax.psum_scatter(grad_w_value, ('dp', 'fsdp'), scatter_dimension=0, tiled...  641 us
    reduce_scatter x1, waiting for transfers between devices, body(): lax.psum_scatter(grad_w_out, ('dp', 'fsdp'), scatter_dimension=0, tiled=T...  625 us
    reduce_scatter x1, waiting for transfers between devices, body(): lax.psum_scatter(grad_w_key, ('dp', 'fsdp'), scatter_dimension=0, tiled=T...  477 us
    reduce_scatter x1, waiting for transfers between devices, body(): lax.psum_scatter(grad_w_gate, ('dp', 'fsdp'), scatter_dimension=0, tiled=...  252 us
    reduce_scatter x1, waiting for transfers between devices, body(): lax.psum_scatter(grad_w_down, ('dp', 'fsdp'), scatter_dimension=0, tiled=...  251 us
    reduce_scatter x1, waiting for transfers between devices, body(): lax.psum_scatter(grad_w_up, ('dp', 'fsdp'), scatter_dimension=0, tiled=True)  225 us
    unnamed x2, blocking collectives  134 us
  transfers between devices with their start and end apart: 14, of which 13 were waited for; matrix products, arithmetic and copies ran while one was open for 3% of the time, Pallas kernels for 0%

commit v1 on v0

v1 whole, which is shorter than its diff:
```python
import functools

import jax
import jax.numpy as jnp
from jax import lax
from jax.experimental import pallas as pl
from jax.experimental.pallas import tpu as pltpu
from jax.sharding import PartitionSpec as P

HQ = 16
HK = 8
HD = 128
EPS = 1e-06
THETA = 1000000.0

bf16 = jnp.bfloat16
f32 = jnp.float32
MESH = pl.DeviceIdType.MESH

ARRAYS = {
    "q": ("n", 8, 1024),
    "g": ("n", 8, 1536),
    "k": ("n", 8, 512),
    "v": ("n", 8, 512),
    "u": ("n", 8, 1536),
    "o": ("c", 16, 1024),
    "d": ("c", 24, 1024),
    "e": ("n", 8, 128),
}
ORDER = {
    "q": "xyz",
    "g": "xyz",
    "k": "yzx",
    "v": "yzx",
    "u": "yzx",
    "o": "zxy",
    "d": "zxy",
    "e": "zxy",
}
NAMES = tuple(ARRAYS)


def full_shape(name):
    kind, rows, cols = ARRAYS[name]
    if kind == "n":
        return (4, 2, 4, 4, 8, cols)
    return (4, 4, 4, rows // 8, 8, cols)


def coords():
    dp = lax.axis_index("dp")
    fs = lax.axis_index("fsdp")
    return {"y": dp // 2, "c": lax.rem(dp, 2), "z": fs // 4, "x": lax.rem(fs, 4)}


def device(pos, axis=None, step=0):
    pos = dict(pos)
    if axis == "c":
        pos["c"] = 1 - pos["c"]
    elif axis is not None:
        pos[axis] = lax.rem(pos[axis] + step + 4, 4)
    return (pos["y"] * 2 + pos["c"], pos["z"] * 4 + pos["x"])


def greet(pos):
    barrier = pltpu.get_barrier_semaphore()
    others = [device(pos, "c")]
    for axis in "xyz":
        others += [device(pos, axis, 1), device(pos, axis, -1)]
    for other in others:
        pl.semaphore_signal(barrier, inc=1, device_id=other, device_id_type=MESH)
    pl.semaphore_wait(barrier, len(others))


def block(ref, name, at, half=None):
    kind, rows, cols = ARRAYS[name]
    part = {axis: pl.ds(at[axis], 1) if axis in at else slice(None) for axis in "yzx"}
    if kind == "n":
        core = slice(None) if half is None else pl.ds(half, 1)
        return ref.at[part["y"], core, part["z"], part["x"]]
    if half is None:
        return ref.at[part["y"], part["z"], part["x"]]
    lanes = pl.ds(half * (cols // 2), cols // 2)
    return ref.at[part["y"], part["z"], part["x"], :, :, lanes]


def gather_kernel(*refs):
    n = len(NAMES)
    own = dict(zip(NAMES, refs[:n]))
    x_in, cot_in, seg_in = refs[n : n + 3]
    full = dict(zip(NAMES, refs[n + 3 : 2 * n + 3]))
    x_all, cot_all, seg_all = refs[2 * n + 3 : 2 * n + 6]
    send, recv, pair_send, pair_recv, local = refs[2 * n + 6 :]
    pos = coords()
    me = pos["c"]
    greet(pos)

    def remote(src, dst, sems, index, target):
        return pltpu.make_async_remote_copy(
            src_ref=src,
            dst_ref=dst,
            send_sem=sems[0].at[index],
            recv_sem=sems[1].at[index],
            device_id=target,
            device_id_type=MESH,
        )

    sibling = device(pos, "c")
    pair_sems = (pair_send, pair_recv)
    pair, kept = {}, {}
    for index, name in enumerate(NAMES):
        kind = ARRAYS[name][0]
        if kind == "n":
            mine = full[name].at[pos["y"], me, pos["z"], pos["x"]]
            kept[name] = pltpu.make_async_copy(own[name].at[me], mine, local.at[index])
            pair[name] = remote(own[name].at[1 - me], mine, pair_sems, index, sibling)
            pair[name].start()
        else:
            mine = full[name].at[pos["y"], pos["z"], pos["x"]]
            kept[name] = pltpu.make_async_copy(own[name], mine, local.at[index])
        kept[name].start()
    late = []
    for index, (src, dst) in enumerate(((x_in, x_all), (cot_in, cot_all), (seg_in, seg_all))):
        copy = remote(src, dst.at[me], pair_sems, n + index, sibling)
        copy.start()
        late.append(copy)
        copy = pltpu.make_async_copy(src, dst.at[me], local.at[n + index])
        copy.start()
        late.append(copy)
    for name in NAMES:
        kept[name].wait()
        if name in pair:
            pair[name].wait()

    sems = (send, recv)
    for phase in range(3):
        copies = {}
        for name in NAMES:
            index = NAMES.index(name)
            axis = ORDER[name][phase]
            at = {a: pos[a] for a in ORDER[name][phase:]}
            src = block(full[name], name, at)
            up = remote(src, src, sems, (index, phase, 0), device(pos, axis, 1))
            down = remote(src, src, sems, (index, phase, 1), device(pos, axis, -1))
            up.start()
            down.start()
            copies[name] = [up, down]
        for name in NAMES:
            index = NAMES.index(name)
            axis = ORDER[name][phase]
            at = {a: pos[a] for a in ORDER[name][phase:]}
            up, down = copies[name]
            up.wait_recv()
            src = block(full[name], name, {**at, axis: lax.rem(pos[axis] + 3, 4)}, 0)
            on_up = remote(src, src, sems, (index, phase, 2), device(pos, axis, 1))
            on_up.start()
            down.wait_recv()
            src = block(full[name], name, {**at, axis: lax.rem(pos[axis] + 1, 4)}, 1)
            on_down = remote(src, src, sems, (index, phase, 3), device(pos, axis, -1))
            on_down.start()
            copies[name] += [on_up, on_down]
        for name in NAMES:
            up, down, on_up, on_down = copies[name]
            on_up.wait_recv()
            on_down.wait_recv()
            for copy in copies[name]:
                copy.wait_send()
    for copy in late:
        copy.wait()


def gather(own, x, cot, seg):
    n = len(NAMES)
    shapes = [jax.ShapeDtypeStruct(full_shape(name), bf16) for name in NAMES]
    shapes += [jax.ShapeDtypeStruct((2,) + a.shape, a.dtype) for a in (x, cot, seg)]
    outs = pl.pallas_call(
        gather_kernel,
        out_shape=shapes,
        in_specs=[pl.BlockSpec(memory_space=pl.ANY)] * (n + 3),
        out_specs=[pl.BlockSpec(memory_space=pl.ANY)] * (n + 3),
        scratch_shapes=[
            pltpu.SemaphoreType.DMA((n, 3, 4)),
            pltpu.SemaphoreType.DMA((n, 3, 4)),
            pltpu.SemaphoreType.DMA((n + 3,)),
            pltpu.SemaphoreType.DMA((n + 3,)),
            pltpu.SemaphoreType.DMA((n + 3,)),
        ],
        compiler_params=pltpu.CompilerParams(collective_id=1, has_side_effects=True),
        name="gather_weights",
    )(*[own[name] for name in NAMES], x, cot, seg)
    return dict(zip(NAMES, outs[:n])), outs[n:]


def merged(name, fixed):
    shape = list(full_shape(name))
    kind = ARRAYS[name][0]
    places = {"y": 0, "z": 2, "x": 3} if kind == "n" else {"y": 0, "z": 1, "x": 2}
    for axis in fixed:
        shape[places[axis]] = 1
    return tuple(shape)


def halved(name, shape):
    kind = ARRAYS[name][0]
    shape = list(shape)
    shape[1 if kind == "n" else -1] //= 2
    return tuple(shape)


def pieces(shape):
    return shape[:-2]


def add_into(dst, sources, shape):
    lead = pieces(shape)
    count = 1
    for extent in lead:
        count *= extent

    def step(i, carry):
        index = []
        rest = i
        for extent in reversed(lead):
            index.append(lax.rem(rest, extent))
            rest = rest // extent
        index = tuple(reversed(index))
        total = sources[0][index].astype(f32)
        for source in sources[1:]:
            total = total + source[index].astype(f32)
        dst[index] = total.astype(dst.dtype)
        return carry

    lax.fori_loop(0, count, step, 0)


def sum_kernel(*refs):
    n = len(NAMES)
    part = dict(zip(NAMES, refs[:n]))
    outs = dict(zip(NAMES, refs[n : 2 * n]))
    scratch = list(refs[2 * n :])
    got, state = {}, {}
    for name in NAMES:
        for phase in range(3):
            got[name, phase] = scratch[:4]
            state[name, phase] = scratch[4]
            scratch = scratch[5:]
    send, recv, pair_send, pair_recv = scratch
    pos = coords()
    me = pos["c"]
    greet(pos)

    def remote(src, dst, sems, index, target):
        return pltpu.make_async_remote_copy(
            src_ref=src,
            dst_ref=dst,
            send_sem=sems[0].at[index],
            recv_sem=sems[1].at[index],
            device_id=target,
            device_id_type=MESH,
        )

    sems = (send, recv)
    current = dict(part)
    for phase in range(3):
        copies = {}
        for name in NAMES:
            index = NAMES.index(name)
            order = ORDER[name][::-1]
            axis = order[phase]
            up, down = device(pos, axis, 1), device(pos, axis, -1)
            ahead, behind = lax.rem(pos[axis] + 1, 4), lax.rem(pos[axis] + 3, 4)
            opposite = lax.rem(pos[axis] + 2, 4)
            cur = current[name]
            far_up, far_down, near_up, near_down = got[name, phase]
            copies[name] = [
                remote(block(cur, name, {axis: opposite}, 0), far_up, sems, (index, phase, 0), up),
                remote(block(cur, name, {axis: opposite}, 1), far_down, sems, (index, phase, 1), down),
                remote(
                    block(cur, name, {axis: ahead}, 1),
                    half_of(near_up, name, 1),
                    sems,
                    (index, phase, 2),
                    up,
                ),
                remote(
                    block(cur, name, {axis: behind}, 0),
                    half_of(near_down, name, 0),
                    sems,
                    (index, phase, 3),
                    down,
                ),
            ]
            for copy in copies[name]:
                copy.start()
        for name in NAMES:
            index = NAMES.index(name)
            order = ORDER[name][::-1]
            axis = order[phase]
            up, down = device(pos, axis, 1), device(pos, axis, -1)
            ahead, behind = lax.rem(pos[axis] + 1, 4), lax.rem(pos[axis] + 3, 4)
            cur = current[name]
            far_up, far_down, near_up, near_down = got[name, phase]
            shape = halved(name, merged(name, order[: phase + 1]))
            copies[name][0].wait_recv()
            add_into(far_up, [far_up, block(cur, name, {axis: ahead}, 0)], shape)
            copy = remote(far_up, half_of(near_up, name, 0), sems, (index, phase, 4), up)
            copy.start()
            copies[name].append(copy)
            copies[name][1].wait_recv()
            add_into(far_down, [far_down, block(cur, name, {axis: behind}, 1)], shape)
            copy = remote(far_down, half_of(near_down, name, 1), sems, (index, phase, 5), down)
            copy.start()
            copies[name].append(copy)
        for name in NAMES:
            order = ORDER[name][::-1]
            axis = order[phase]
            cur = current[name]
            near_up, near_down = got[name, phase][2:]
            for copy in copies[name][2:]:
                copy.wait_recv()
            shape = merged(name, order[: phase + 1])
            add_into(state[name, phase], [near_up, near_down, block(cur, name, {axis: pos[axis]})], shape)
            for copy in copies[name]:
                copy.wait_send()
            current[name] = state[name, phase]
    sibling = device(pos, "c")
    pairs = []
    for index, name in enumerate(NAMES):
        cur = current[name]
        if ARRAYS[name][0] == "n":
            copy = remote(
                cur.at[0, 1 - me, 0, 0], outs[name].at[me], (pair_send, pair_recv), index, sibling
            )
            copy.start()
            pairs.append(copy)
            outs[name][me] = cur[0, me, 0, 0]
        else:
            outs[name][...] = cur[0, 0, 0]
    for copy in pairs:
        copy.wait()


def half_of(ref, name, half):
    kind, rows, cols = ARRAYS[name]
    if kind == "n":
        return ref.at[:, pl.ds(half, 1)]
    return ref.at[:, :, :, :, :, pl.ds(half * (cols // 2), cols // 2)]


def reduce_all(part):
    n = len(NAMES)
    scratch = []
    for name in NAMES:
        order = ORDER[name][::-1]
        for phase in range(3):
            shape = merged(name, order[: phase + 1])
            half = halved(name, shape)
            scratch += [pltpu.VMEM(half, bf16), pltpu.VMEM(half, bf16)]
            scratch += [pltpu.VMEM(shape, bf16), pltpu.VMEM(shape, bf16)]
            scratch += [pltpu.VMEM(shape, f32 if phase == 2 else bf16)]
    shapes = []
    for name in NAMES:
        kind, rows, cols = ARRAYS[name]
        shape = (2, 8, cols) if kind == "n" else (rows // 8, 8, cols)
        shapes.append(jax.ShapeDtypeStruct(shape, f32))
    outs = pl.pallas_call(
        sum_kernel,
        out_shape=shapes,
        in_specs=[pl.BlockSpec(memory_space=pltpu.VMEM)] * n,
        out_specs=[pl.BlockSpec(memory_space=pltpu.VMEM)] * n,
        scratch_shapes=scratch
        + [
            pltpu.SemaphoreType.DMA((n, 3, 6)),
            pltpu.SemaphoreType.DMA((n, 3, 6)),
            pltpu.SemaphoreType.DMA((n,)),
            pltpu.SemaphoreType.DMA((n,)),
        ],
        compiler_params=pltpu.CompilerParams(
            collective_id=2, has_side_effects=True, vmem_limit_bytes=60 << 20
        ),
        name="sum_gradients",
    )(*[part[name] for name in NAMES])
    return dict(zip(NAMES, outs))


def contract(left, right, left_dim, right_dim):
    return lax.dot_general(
        left, right, (((left_dim,), (right_dim,)), ((), ())), preferred_element_type=f32
    )


def inverse_rms(vector):
    return lax.rsqrt(jnp.mean(vector * vector, axis=-1, keepdims=True) + EPS)


def norm_backward(grad_in, unit_vec, inverse, gain_vec):
    scaled = grad_in * gain_vec
    return inverse * (scaled - unit_vec * jnp.mean(scaled * unit_vec, axis=-1, keepdims=True))


def rotate(vector, cos_part, sin_part):
    first, second = vector[..., : HD // 2], vector[..., HD // 2 :]
    return jnp.concatenate(
        [first * cos_part - second * sin_part, second * cos_part + first * sin_part], axis=-1
    )


def unrotate(vector, cos_part, sin_part):
    return rotate(vector, cos_part, -sin_part)


def from_sibling(value):
    size = lax.axis_size("fsdp")
    total = lax.axis_size("dp") * size
    pairs = []
    for i in range(total):
        dp, fs = i // size, i % size
        pairs.append((i, (dp ^ 1) * size + fs))
    return lax.ppermute(value, ("dp", "fsdp"), pairs)


def split_columns(weight, width):
    rows, cols = weight.shape
    halves = weight.astype(bf16).reshape(rows, cols // (2 * width), 2, width)
    return halves.transpose(2, 0, 1, 3).reshape(2, rows, cols // 2)


def join_columns(halves, width):
    _, rows, cols = halves.shape
    blocks = halves.reshape(2, rows, cols // width, width)
    return blocks.transpose(1, 2, 0, 3).reshape(rows, 2 * cols)


def body(
    tokens, segment, norm_gain, w_query, w_key, w_value, query_gain, key_gain, w_out, mlp_gain,
    w_gate, w_up, w_down, cotangent,
):
    core = lax.rem(lax.axis_index("dp"), 2)
    first_row = jnp.arange(8)[:, None] == 0
    gains = jnp.concatenate(
        [
            norm_gain[:, None],
            mlp_gain[:, None],
            jnp.where(first_row, query_gain[0], 0.0),
            jnp.where(first_row, key_gain[0], 0.0),
            jnp.zeros((8, 124), f32),
        ],
        axis=1,
    ).astype(bf16)
    own = {
        "q": split_columns(w_query, 256),
        "g": split_columns(w_gate, 384),
        "k": split_columns(w_key, 128),
        "v": split_columns(w_value, 128),
        "u": split_columns(w_up, 384),
        "o": w_out.astype(bf16).reshape(2, 8, 1024),
        "d": w_down.astype(bf16).reshape(3, 8, 1024),
        "e": jnp.stack([gains, gains]),
    }
    seg_rows = jnp.broadcast_to(segment, (8, 128))
    full, (x_pair, cot_pair, seg_pair) = gather(own, tokens, cotangent, seg_rows)
    wq = full["q"].reshape(1024, 1024)
    wk = full["k"].reshape(1024, 512)
    wv = full["v"].reshape(1024, 512)
    wg = full["g"].reshape(1024, 1536)
    wu = full["u"].reshape(1024, 1536)
    wo = full["o"].reshape(1024, 1024)
    wd = full["d"].reshape(1536, 1024)
    columns = full["e"].reshape(1024, 128)[:, :4].astype(f32).T
    gain_in, gain_mid = columns[0], columns[1]
    gain_query, gain_key = columns[2].reshape(128, 8)[:, 0], columns[3].reshape(128, 8)[:, 0]

    rows = 256
    seg_ids = seg_pair[:, 0, :]
    index = jnp.arange(128, dtype=jnp.int32)
    same = seg_ids[:, :, None] == seg_ids[:, None, :]
    allowed = same & (index[None, :] <= index[:, None])[None]
    position = jnp.sum((same & (index[None, :] < index[:, None])[None]).astype(jnp.int32), axis=2)
    inv_freq = THETA ** (-jnp.arange(HD // 2, dtype=f32) * 2.0 / HD)
    angles = position.reshape(rows).astype(f32)[:, None] * inv_freq[None, :]
    cos_part = jnp.cos(angles)[:, None, :]
    sin_part = jnp.sin(angles)[:, None, :]
    scale = HD ** (-0.5)
    nq, nk, group = HQ // 2, HK // 2, HQ // HK

    x = x_pair.reshape(rows, 1024).astype(f32)
    cot = cot_pair.reshape(rows, 1024)
    inv_in = inverse_rms(x)
    unit_in = x * inv_in
    normed = (unit_in * gain_in).astype(bf16)
    q_raw = jnp.dot(normed, wq, preferred_element_type=f32).reshape(rows, nq, HD)
    k_raw = jnp.dot(normed, wk, preferred_element_type=f32).reshape(rows, nk, HD)
    values = jnp.dot(normed, wv, preferred_element_type=f32).astype(bf16).reshape(2, 128, nk, HD)
    inv_q = inverse_rms(q_raw)
    unit_q = q_raw * inv_q
    inv_k = inverse_rms(k_raw)
    unit_k = k_raw * inv_k
    q_rot = rotate(unit_q * gain_query, cos_part, sin_part).astype(bf16)
    k_rot = rotate(unit_k * gain_key, cos_part, sin_part).astype(bf16).reshape(2, 128, nk, HD)
    q_group = q_rot.reshape(2, 128, nk, group, HD)
    scores = jnp.einsum("bqhgd,bkhd->bhgqk", q_group, k_rot, preferred_element_type=f32) * scale
    masked = jnp.where(allowed[:, None, None], scores, -1e30)
    exp_terms = jnp.exp(masked - jnp.max(masked, axis=-1, keepdims=True))
    prob_full = exp_terms / jnp.sum(exp_terms, axis=-1, keepdims=True)
    prob_low = prob_full.astype(bf16)
    attended = (
        jnp.einsum("bhgqk,bkhd->bqhgd", prob_low, values, preferred_element_type=f32)
        .astype(bf16)
        .reshape(rows, nq * HD)
    )
    out_part = jnp.dot(attended, wo, preferred_element_type=f32)
    hidden = x + (out_part + from_sibling(out_part))
    inv_mid = inverse_rms(hidden)
    unit_mid = hidden * inv_mid
    mid_low = (unit_mid * gain_mid).astype(bf16)
    gate = jnp.dot(mid_low, wg, preferred_element_type=f32)
    up = jnp.dot(mid_low, wu, preferred_element_type=f32)
    sig = jax.nn.sigmoid(gate)
    act = gate * sig
    mixed = (act * up).astype(bf16)
    down_part = jnp.dot(mixed, wd, preferred_element_type=f32).reshape(2, 128, 1024)
    hidden_pair = hidden.reshape(2, 128, 1024)
    down_own = lax.dynamic_index_in_dim(down_part, core, 0, False)
    down_other = from_sibling(lax.dynamic_index_in_dim(down_part, 1 - core, 0, False))
    layer_out = (
        lax.dynamic_index_in_dim(hidden_pair, core, 0, False) + (down_own + down_other)
    ).astype(bf16)

    grad = {}
    grad["d"] = contract(mixed, cot, 0, 0)
    d_mixed = contract(cot, wd, 1, 1)
    d_gate = (d_mixed * up * sig * (1.0 + gate * (1.0 - sig))).astype(bf16)
    d_up = (d_mixed * act).astype(bf16)
    grad["g"] = contract(mid_low, d_gate, 0, 0)
    grad["u"] = contract(mid_low, d_up, 0, 0)
    mid_part = contract(d_gate, wg, 1, 1) + contract(d_up, wu, 1, 1)
    grad_mlp_gain = jnp.sum(mid_part * unit_mid, axis=0)
    d_mid = mid_part + from_sibling(mid_part)
    d_res = cot.astype(f32) + norm_backward(d_mid, unit_mid, inv_mid, gain_mid)
    d_res_low = d_res.astype(bf16)
    grad["o"] = contract(attended, d_res_low, 0, 0)
    d_attn = contract(d_res_low, wo, 1, 1).astype(bf16).reshape(2, 128, nk, group, HD)
    d_probs = jnp.einsum("bqhgd,bkhd->bhgqk", d_attn, values, preferred_element_type=f32)
    d_values = (
        jnp.einsum("bhgqk,bqhgd->bkhd", prob_low, d_attn, preferred_element_type=f32)
        .astype(bf16)
        .reshape(rows, nk * HD)
    )
    d_scores = (
        prob_full * (d_probs - jnp.sum(d_probs * prob_full, axis=-1, keepdims=True))
    ).astype(bf16)
    d_qrot = (
        jnp.einsum("bhgqk,bkhd->bqhgd", d_scores, k_rot, preferred_element_type=f32) * scale
    ).reshape(rows, nq, HD)
    d_krot = (
        jnp.einsum("bhgqk,bqhgd->bkhd", d_scores, q_group, preferred_element_type=f32) * scale
    ).reshape(rows, nk, HD)
    d_qunit = unrotate(d_qrot, cos_part, sin_part)
    d_kunit = unrotate(d_krot, cos_part, sin_part)
    grad_query_gain = jnp.sum(d_qunit * unit_q, axis=(0, 1))
    grad_key_gain = jnp.sum(d_kunit * unit_k, axis=(0, 1))
    d_qraw = norm_backward(d_qunit, unit_q, inv_q, gain_query).astype(bf16).reshape(rows, nq * HD)
    d_kraw = norm_backward(d_kunit, unit_k, inv_k, gain_key).astype(bf16).reshape(rows, nk * HD)
    grad["q"] = contract(normed, d_qraw, 0, 0)
    grad["k"] = contract(normed, d_kraw, 0, 0)
    grad["v"] = contract(normed, d_values, 0, 0)
    in_part = contract(d_qraw, wq, 1, 1) + contract(d_kraw, wk, 1, 1) + contract(d_values, wv, 1, 1)
    grad_norm_gain = jnp.sum(in_part * unit_in, axis=0)
    in_pair = in_part.reshape(2, 128, 1024)

    def mine(value):
        return lax.dynamic_index_in_dim(value.reshape(2, 128, -1), core, 0, False)

    in_other = from_sibling(lax.dynamic_index_in_dim(in_pair, 1 - core, 0, False))
    d_normed = mine(in_part) + in_other
    input_grad = mine(d_res) + norm_backward(d_normed, mine(unit_in), mine(inv_in), gain_in)

    spread = jnp.arange(8)[None, :, None] == 0
    grad["e"] = jnp.concatenate(
        [
            grad_norm_gain[:, None],
            grad_mlp_gain[:, None],
            jnp.where(spread, grad_query_gain[:, None, None], 0.0).reshape(1024, 1),
            jnp.where(spread, grad_key_gain[:, None, None], 0.0).reshape(1024, 1),
            jnp.zeros((1024, 124), f32),
        ],
        axis=1,
    )
    part = {name: grad[name].astype(bf16).reshape(full_shape(name)) for name in NAMES}
    total = reduce_all(part)
    gain_grads = total["e"][0] + total["e"][1]
    return (
        layer_out,
        input_grad,
        gain_grads[:, 0],
        join_columns(total["q"], 256),
        join_columns(total["k"], 128),
        join_columns(total["v"], 128),
        gain_grads[:1, 2],
        gain_grads[:1, 3],
        total["o"].reshape(16, 1024),
        gain_grads[:, 1],
        join_columns(total["g"], 384),
        join_columns(total["u"], 384),
        total["d"].reshape(24, 1024),
    )


def solution(mesh):
    rows = P(("dp", "fsdp"), None)
    flat = P(("dp", "fsdp"))
    return jax.shard_map(
        body,
        mesh=mesh,
        in_specs=(rows, rows, flat, rows, rows, rows, flat, flat, rows, flat, rows, rows, rows, rows),
        out_specs=(rows, rows, flat, rows, rows, rows, flat, flat, rows, flat, rows, rows, rows),
        check_vma=False,
    )
```

time: 3790 us -> 316 us (0.08)
  waiting for transfers between devices: 3490 us -> 0.01 us
  Pallas kernels: 0 us -> 161 us
  blocking collectives: 134 us -> 0 us
  matrix products: 97 us -> 49.7 us
    reduce_scatter x7 -> x0, waiting for transfers between devices: 3120 us -> none  [the longest x1 651 us: body(): lax.psum_scatter(grad_w_query, ('dp', 'fsdp'), scatter_dimension=0, tiled...]
    all_gather x7 -> x0, waiting for transfers between devices: 365 us -> none  [the longest x1 66 us: body(): lax.all_gather(low_mlp[1], ('dp', 'fsdp'), axis=0, tiled=True)]
    pallas_call x0 -> x2, Pallas kernels: none -> 161 us  [the longest x1 84.9 us: reduce_all(): pl.pallas_call(sum_kernel, out_shape=shapes, in_specs=[pl.BlockSpec(memor...]
    unnamed x2 -> x0, blocking collectives: 134 us -> none
  transfers between devices with their start and end apart: 14 -> 4, of which waited for: 13 -> 0; matrix products, arithmetic and copies ran while one was open for 3% -> 8% of each run, Pallas kernels for 0% -> 27%
where the time goes in v1:
time: 316 us; the launch traced here: 314 us
  Pallas kernels  161 us (51%)
  local copies, waits for them, and re-layouts  58.2 us (18%)
  matrix products  49.7 us (16%)
  other arithmetic  34.7 us (11%)
  starting transfers between devices  7.86 us (2%)
    pallas_call x1, Pallas kernels, reduce_all(): pl.pallas_call(sum_kernel, out_shape=shapes, in_specs=[pl.BlockSpec(memor...  84.9 us
    pallas_call x1, Pallas kernels, gather(): pl.pallas_call(gather_kernel, out_shape=shapes, in_specs=[pl.BlockSpec(me...  76.4 us
    dot_general x14, matrix products, contract(): lax.dot_general(left, right, (((left_dim,), (right_dim,)), ((), ())), pre...  24.6 us
    concatenate x8, local copies, waits for them, and re-layouts, rotate(): jnp.concatenate([first * cos_part - second * sin_part, second * cos_part...  9.9 us
    unnamed x83, local copies, waits for them, and re-layouts  8.45 us
    ppermute x4, starting transfers between devices, from_sibling(): return lax.ppermute(value, ('dp', 'fsdp'), pairs)  7.86 us
    transpose x5, local copies, waits for them, and re-layouts, join_columns(): return blocks.transpose(1, 2, 0, 3).reshape(rows, 2 * cols)  7.3 us
  transfers between devices with their start and end apart: 4, of which 0 were waited for; matrix products, arithmetic and copies ran while one was open for 8% of the time, Pallas kernels for 27%

profile of v1, /device:TPU:1, one launch (start us, length us, event | category | flops | bytes accessed | tf_op | source)
XLA Modules:
  0.0 314.3 jit_solution(5838513032959270843)
XLA Ops:
  11.0 1.5 convert_bitcast_fusion.refs_6_
  12.6 1.5 convert_bitcast_fusion.1.refs_5_
  14.6 1.2 broadcast_in_dim.107.refs_10_
  15.9 76.4 %gather_weights.1 = (bf16[4,2,4,4,8,1024]{5,4,3,2,1,0:T(8,128)(2,1)}, bf16[4,2,4,4,8,1536]{5,4,3,2,1,0:T(8,128)(2,1)}, bf16[4,2,4,4,8,512]{5,4,3,2,1,0:T(8,128)(...) custom-call(bf16[2,8,1024]{2,1,0:T(8,128)(2,1)} %bitcast.323, ...), custom_call_target="tpu_custom_call" | custom-call | tf_op jit(solution)/shard_map/gather_weights/pallas_call | solution.py:176
  97.7 1.3 multiply_reduce_fusion.9
  102.8 1.6 concatenate.57
  104.4 1.8 copy.101
  106.8 1.8 copy.102
  108.6 2.6 copy.103
  111.2 2.3 multiply_reduce_fusion.6
  119.0 1.5 compare_and_fusion.1
  121.7 3.7 %fusion.47 = (f32[2,4,2,128]{3,2,1,0:T(2,128)}, f32[2,4,2,128,128]{3,4,2,1,0:T(8,128)}) fusion(pred[2,128,128]{1,2,0:T(8,128)(4,1)} %compare_and_fusion.1, bf16[2,128,4,2,64]{4,1,3,2,0:T(8,128)(2,1)} %copy.105, bf16[2,128,4,2,64]{4,1,3,2,0:T(8,128)(2,1)} %copy.104, bf16[2,128,4,64]{3,1,2,0:T(8,128)(2,1)} %copy.102, bf16[2,128,4,64]{3,1,2,0:T(8,128)(2,1)} %copy.101), kind=kOutput, calls=%fused_computation.148 | convolution fusion | flops 69730432 | bytes 1875968 | tf_op jit(solution)/shard_map/sub | solution.py:503
  125.4 2.8 fusion.7
  128.2 1.3 copy.108
  129.9 3.5 %fusion.48 = f32[256,1024]{1,0:T(8,128)} fusion(bf16[256,1024]{1,0:T(8,128)(2,1)S(1)} %reshape.640, bf16[1024,1024]{1,0:T(8,128)(2,1)} %bitcast.289), kind=kOutput, calls=%fused_computation.149 | convolution fusion | flops 536870912 | bytes 3670016 | tf_op jit(solution)/shard_map/dot_general | solution.py:511
  133.4 7.2 %collective-permute-start = (f32[256,1024]{1,0:T(8,128)}, f32[256,1024]{1,0:T(8,128)}, u32[]{:S(2)}, u32[]{:S(2)}) collective-permute-start(f32[256,1024]{1,0:T(8,128)} %fusion.48), channel_id=1, source_target_pairs={{0,16},{1,17},{2,18},{3,19},{4,20},{5,21},{6,22},{7,23},{8,24},{9,... | collective-permute-start | bytes 3145736 | tf_op jit(solution)/shard_map/ppermute | solution.py:419
  142.3 2.9 fusion.51
  145.3 1.9 multiply_reduce_fusion.5
  149.6 1.6 multiply_convert_fusion
  155.1 2.7 convolution_convert_fusion.1
  157.9 2.7 convolution_convert_fusion.2
  160.6 2.7 convolution_convert_fusion
  166.7 1.6 convolution_convert_fusion.8
  168.3 2.2 reshape.648
  170.5 2.0 copy.114
  172.5 1.8 multiply_reduce_fusion.3
  175.6 1.3 fusion.9
  176.9 1.4 fusion.4
  178.3 3.1 fusion.11
  181.4 3.2 %convolution_convert_fusion.3 = bf16[1024,1024]{1,0:T(8,128)(2,1)} fusion(bf16[256,1024]{1,0:T(8,128)(2,1)} %copy-done.7, f32[256,1024]{1,0:T(8,128)S(1)} %multiply_add_fusion), kind=kOutput, calls=%fused_computation.4 | convolution fusion | flops 538181632 | bytes 3670016 | tf_op jit(solution)/shard_map/dot_general | solution.py:387
  184.6 2.0 copy.113
  186.6 2.3 reshape.651
  192.0 2.3 copy.112
  194.3 3.0 reshape.649
  197.3 1.3 multiply_subtract_fusion
  201.1 1.3 multiply_convert_fusion.7
  202.4 1.4 multiply_convert_fusion.3
  203.9 2.1 convolution_convert_fusion.4
  206.7 1.5 convolution_convert_fusion.5
  208.2 1.5 convolution_convert_fusion.6
  214.0 1.5 concatenate.67.refs_7_
  215.5 84.9 %sum_gradients.1 = (f32[2,8,1024]{2,1,0:T(8,128)}, f32[2,8,1536]{2,1,0:T(8,128)}, f32[2,8,512]{2,1,0:T(8,128)}, f32[2,8,512]{2,1,0:T(8,128)}, f32[2,8,1536]{2,1,...) custom-call(bf16[4,2,4,4,8,1024]{5,4,3,2,1,0:T(8,128)(2,1)} %bitcast.291, ...), custom_call_target="tpu_custom_call" | custom-call | tf_op jit(solution)/shard_map/sum_gradients/pallas_call | solution.py:366
  300.5 1.5 copy.123
  302.0 1.5 copy.122
  303.5 1.5 copy.119
  305.0 1.4 copy.120
  306.4 1.4 copy.121
  311.0 2.0 fusion.18
  (175 shorter events, 54.3 us)
Async XLA Ops:
  92.3 3.7 %copy-start.10 = (bf16[4,2,4,4,8,512]{5,4,3,2,1,0:T(8,128)(2,1)S(1)}, bf16[4,2,4,4,8,512]{5,4,3,2,1,0:T(8,128)(2,1)}, u32[]{:S(2)}) copy-start(bf16[4,2,4,4,8,512]{5,4,3,2,1,0:T(8,128)(2,1)} %get-tuple-element.36) | copy-start | bytes 3145732
  92.3 4.3 %copy-start.4 = (bf16[2,128,1024]{2,1,0:T(8,128)(2,1)S(1)}, bf16[2,128,1024]{2,1,0:T(8,128)(2,1)}, u32[]{:S(2)}) copy-start(bf16[2,128,1024]{2,1,0:T(8,128)(2,1)} %get-tuple-element.32) | copy-start | bytes 1572868
  96.0 1.7 copy-start.35
  99.0 9.6 %copy-start.2 = (bf16[4,2,4,4,8,1024]{5,4,3,2,1,0:T(8,128)(2,1)S(1)}, bf16[4,2,4,4,8,1024]{5,4,3,2,1,0:T(8,128)(2,1)}, u32[]{:S(2)}) copy-start(bf16[4,2,4,4,8,1024]{5,4,3,2,1,0:T(8,128)(2,1)} %get-tuple-element.37) | copy-start | bytes 6291460
  99.2 12.0 %copy-start.29 = (f32[128]{0:T(128)}, f32[128]{0:T(128)S(1)}, u32[]{:S(2)}) copy-start(f32[128]{0:T(128)S(1)} %slice_reduce_fusion.1) | copy-start | bytes 1540
  100.0 0.6 copy-start.28
  113.8 1.2 copy-start.33
  114.0 6.5 %copy-start.12 = (bf16[4,2,4,4,8,512]{5,4,3,2,1,0:T(8,128)(2,1)S(1)}, bf16[4,2,4,4,8,512]{5,4,3,2,1,0:T(8,128)(2,1)}, u32[]{:S(2)}) copy-start(bf16[4,2,4,4,8,512]{5,4,3,2,1,0:T(8,128)(2,1)} %get-tuple-element.34) | copy-start | bytes 3145732
  120.9 4.5 %copy-start.18 = (bf16[2,128,4,2,64]{4,1,3,2,0:T(8,128)(2,1)S(1)}, bf16[2,128,4,2,64]{4,1,3,2,0:T(8,128)(2,1)}, u32[]{:S(2)}) copy-start(bf16[2,128,4,2,64]{4,1,3,2,0:T(8,128)(2,1)} %copy.104) | copy-start | bytes 786436
  120.9 4.5 %copy-start.20 = (bf16[2,128,4,2,64]{4,1,3,2,0:T(8,128)(2,1)S(1)}, bf16[2,128,4,2,64]{4,1,3,2,0:T(8,128)(2,1)}, u32[]{:S(2)}) copy-start(bf16[2,128,4,2,64]{4,1,3,2,0:T(8,128)(2,1)} %copy.105) | copy-start | bytes 786436
  121.7 3.7 %copy-start.23 = (bf16[2,128,4,64]{3,1,2,0:T(8,128)(2,1)S(1)}, bf16[2,128,4,64]{3,1,2,0:T(8,128)(2,1)}, u32[]{:S(2)}) copy-start(bf16[2,128,4,64]{3,1,2,0:T(8,128)(2,1)} %copy.101) | copy-start | bytes 393220
  129.9 15.3 %copy-start.7 = (bf16[256,1024]{1,0:T(8,128)(2,1)}, bf16[256,1024]{1,0:T(8,128)(2,1)S(1)}, u32[]{:S(2)}) copy-start(bf16[256,1024]{1,0:T(8,128)(2,1)S(1)} %reshape.640) | copy-start | bytes 1572868
  129.9 12.4 %copy-start.5 = (bf16[2,128,1024]{2,1,0:T(8,128)(2,1)S(1)}, bf16[2,128,1024]{2,1,0:T(8,128)(2,1)}, u32[]{:S(2)}) copy-start(bf16[2,128,1024]{2,1,0:T(8,128)(2,1)} %get-tuple-element.42) | copy-start | bytes 1572868
  133.4 11.8 %collective-permute-start = (f32[256,1024]{1,0:T(8,128)}, f32[256,1024]{1,0:T(8,128)}, u32[]{:S(2)}, u32[]{:S(2)}) collective-permute-start(f32[256,1024]{1,0:T(8,128)} %fusion.48), channel_id=1, source_target_pairs={{0,16},{1,17},{2,18},{3,19},{4,20},{5,21},{6,22},{7,23},{8,24},{9,... | collective-permute-start | bytes 3145736 | tf_op jit(solution)/shard_map/ppermute | solution.py:419
  145.2 2.0 copy-start.26
  145.2 2.5 copy-start
  147.8 1.9 copy-start.39
  152.2 1.9 copy-start.15
  153.3 10.9 %collective-permute-start.2 = (f32[256,1024]{1,0:T(8,128)S(1)}, f32[256,1024]{1,0:T(8,128)S(1)}, u32[]{:S(2)}, u32[]{:S(2)}) collective-permute-start(f32[256,1024]{1,0:T(8,128)S(1)} %convolution_add_fusion.2), channel_id=1, source_target_pairs={{0,16},{1,17},{2,18},{3,19},{4,20},{5,21},{6,22},{7,23},{8,24},{9,... | collective-permute-start | bytes 3145736 | tf_op jit(solution)/shard_map/ppermute | solution.py:419
  157.9 5.5 %collective-permute-start.1 = (f32[128,1024]{1,0:T(8,128)S(1)}, f32[128,1024]{1,0:T(8,128)S(1)}, u32[]{:S(2)}, u32[]{:S(2)}) collective-permute-start(f32[128,1024]{1,0:T(8,128)S(1)} %dynamic-slice_bitcast_fusion.1), channel_id=1, source_target_pairs={{0,16},{1,17},{2,18},{3,19},{4,20},{5,21},{6,22},{7,23},{8,24},{9,... | collective-permute-start | bytes 1572872 | tf_op jit(solution)/shard_map/ppermute | solution.py:419
  163.3 1.8 copy-start.6
  165.1 1.6 copy-start.1
  172.5 1.9 copy-start.22
  172.5 1.9 copy-start.31
  174.4 1.0 copy-start.19
  174.4 1.2 copy-start.21
  174.4 2.4 copy-start.24
  184.6 6.1 %copy-start.30 = (f32[128]{0:T(128)S(1)}, f32[128]{0:T(128)}, u32[]{:S(2)}) copy-start(f32[128]{0:T(128)} %copy-done.29) | copy-start | bytes 1540
  190.0 0.7 copy-start.16
  190.0 1.9 copy-start.17
  194.3 5.2 %copy-start.34 = (f32[128]{0:T(128)S(1)}, f32[128]{0:T(128)}, u32[]{:S(2)}) copy-start(f32[128]{0:T(128)} %copy-done.33) | copy-start | bytes 1540
  198.7 0.8 copy-start.8
  198.7 1.1 copy-start.9
  203.9 2.1 copy-start.3
  206.7 2.9 copy-start.11
  209.7 1.2 copy-start.13
  209.7 1.2 copy-start.36
  210.9 1.9 copy-start.37
  210.9 2.6 copy-start.32
  212.2 97.5 %collective-permute-start.3 = (f32[128,1024]{1,0:T(8,128)}, f32[128,1024]{1,0:T(8,128)}, u32[]{:S(2)}, u32[]{:S(2)}) collective-permute-start(f32[128,1024]{1,0:T(8,128)} %dynamic-slice_bitcast_fusion), channel_id=1, source_target_pairs={{0,16},{1,17},{2,18},{3,19},{4,20},{5,21},{6,22},{7,23},{8,24},{9,... | collective-permute-start | bytes 1572872 | tf_op jit(solution)/shard_map/ppermute | solution.py:419
  215.5 94.2 %copy-start.14 = (f32[2,128,1024]{2,1,0:T(8,128)S(1)}, f32[2,128,1024]{2,1,0:T(8,128)}, u32[]{:S(2)}) copy-start(f32[2,128,1024]{2,1,0:T(8,128)} %get-tuple-element.74) | copy-start | bytes 3145732
  300.4 10.6 %copy-start.38 = (f32[128]{0:T(128)S(1)}, f32[128]{0:T(128)}, u32[]{:S(2)}) copy-start(f32[128]{0:T(128)} %fusion.37) | copy-start | bytes 1540
  309.7 3.3 %copy-start.27 = (f32[2,8,1024]{2,1,0:T(8,128)S(1)}, f32[2,8,1024]{2,1,0:T(8,128)}, u32[]{:S(2)}) copy-start(f32[2,8,1024]{2,1,0:T(8,128)} %get-tuple-element.47) | copy-start | bytes 196612
  309.7 3.9 %copy-start.25 = (f32[3,8,1024]{2,1,0:T(8,128)S(1)}, f32[3,8,1024]{2,1,0:T(8,128)}, u32[]{:S(2)}) copy-start(f32[3,8,1024]{2,1,0:T(8,128)} %get-tuple-element.50) | copy-start | bytes 294916

commit v2 on v0

v2 whole, which is shorter than its diff:
```python
import types

import jax
import jax.numpy as jnp
from jax import lax
from jax.experimental import pallas as pl
from jax.experimental.pallas import tpu as pltpu
from jax.sharding import PartitionSpec as P

HD = 128
EPS = 1e-06
LOG_THETA = 13.815510557964274
SCALE = HD ** (-0.5)

bf16 = jnp.bfloat16
f32 = jnp.float32
MESH = pl.DeviceIdType.MESH

ARRAYS = {
    "q": ("n", 8, 1024, 256),
    "k": ("n", 8, 512, 128),
    "v": ("n", 8, 512, 128),
    "o": ("c", 16, 1024, 0),
    "e": ("n", 8, 128, 0),
    "g": ("n", 8, 1536, 384),
    "u": ("n", 8, 1536, 384),
    "d": ("c", 24, 1024, 0),
}
ORDER = {"q": "xyz", "g": "xyz", "k": "yzx", "v": "yzx", "u": "yzx", "o": "zxy", "d": "zxy", "e": "zxy"}
NAMES = tuple(ARRAYS)
ATTN = ("q", "k", "v", "o", "e")
MLP = ("g", "u", "d")
SPLIT = tuple(name for name in NAMES if ARRAYS[name][0] == "n")


def full_shape(name):
    kind, rows, cols, _ = ARRAYS[name]
    if kind == "n":
        return (4, 2, 4, 4, 8, cols)
    return (4, 4, 4, rows // 8, 8, cols)


def coords():
    dp = lax.axis_index("dp")
    fs = lax.axis_index("fsdp")
    return {"y": dp // 2, "c": lax.rem(dp, 2), "z": fs // 4, "x": lax.rem(fs, 4)}


def device(pos, axis=None, step=0):
    pos = dict(pos)
    if axis == "c":
        pos["c"] = 1 - pos["c"]
    elif axis is not None:
        pos[axis] = lax.rem(pos[axis] + step + 4, 4)
    return (pos["y"] * 2 + pos["c"], pos["z"] * 4 + pos["x"])


def greet(pos):
    barrier = pltpu.get_barrier_semaphore()
    others = [device(pos, "c")]
    for axis in "xyz":
        others += [device(pos, axis, 1), device(pos, axis, -1)]
    for other in others:
        pl.semaphore_signal(barrier, inc=1, device_id=other, device_id_type=MESH)
    pl.semaphore_wait(barrier, len(others))


def block(ref, name, at, half=None):
    kind, _, cols, _ = ARRAYS[name]
    part = {axis: pl.ds(at[axis], 1) if axis in at else slice(None) for axis in "yzx"}
    if kind == "n":
        core = slice(None) if half is None else pl.ds(half, 1)
        return ref.at[part["y"], core, part["z"], part["x"]]
    if half is None:
        return ref.at[part["y"], part["z"], part["x"]]
    lanes = pl.ds(half * (cols // 2), cols // 2)
    return ref.at[part["y"], part["z"], part["x"], :, :, lanes]


def half_of(ref, name, half):
    kind, _, cols, _ = ARRAYS[name]
    if kind == "n":
        return ref.at[:, pl.ds(half, 1)]
    return ref.at[:, :, :, :, :, pl.ds(half * (cols // 2), cols // 2)]


def merged(name, fixed):
    shape = list(full_shape(name))
    places = {"y": 0, "z": 2, "x": 3} if ARRAYS[name][0] == "n" else {"y": 0, "z": 1, "x": 2}
    for axis in fixed:
        shape[places[axis]] = 1
    return tuple(shape)


def halved(name, shape):
    shape = list(shape)
    shape[1 if ARRAYS[name][0] == "n" else -1] //= 2
    return tuple(shape)


def add_into(dst, sources, shape):
    lead = shape[:-3]
    count = 1
    for extent in lead:
        count *= extent

    def step(i, carry):
        index, rest = [], i
        for extent in reversed(lead):
            index.append(lax.rem(rest, extent))
            rest = rest // extent
        index = tuple(reversed(index))
        total = sources[0][index].astype(f32)
        for source in sources[1:]:
            total = total + source[index].astype(f32)
        dst[index] = total.astype(dst.dtype)
        return carry

    lax.fori_loop(0, count, step, 0)


def dot(left, right):
    return jnp.dot(left, right, preferred_element_type=f32)


def dot_nt(left, right):
    return lax.dot_general(left, right, (((1,), (1,)), ((), ())), preferred_element_type=f32)


def dot_tn(left, right):
    return lax.dot_general(left, right, (((0,), (0,)), ((), ())), preferred_element_type=f32)


def inverse_rms(vector):
    return lax.rsqrt(jnp.mean(vector * vector, axis=-1, keepdims=True) + EPS)


def norm_backward(grad_in, unit_vec, inverse, gain_vec):
    scaled = grad_in * gain_vec
    return inverse * (scaled - unit_vec * jnp.mean(scaled * unit_vec, axis=-1, keepdims=True))


def lanes_at(start, size):
    return pl.ds(pl.multiple_of(start, 128), size)


def loop(count, body):
    def step(i, carry):
        body(i)
        return carry

    lax.fori_loop(0, count, step, 0)


W = {name: (full_shape(name), bf16) for name in NAMES}
STAGE = {name: ((8, ARRAYS[name][2]), bf16) for name in SPLIT}
FIN = {name: ((2, 8, ARRAYS[name][2]), f32) for name in SPLIT}
RX = {name: ((8, ARRAYS[name][2]), f32) for name in SPLIT}
FAR, NEAR = {}, {}
for _name in NAMES:
    for _phase in range(3):
        _shape = merged(_name, ORDER[_name][::-1][: _phase + 1])
        for _way in range(2):
            FAR[_name, _phase, _way] = (halved(_name, _shape), bf16)
            NEAR[_name, _phase, _way] = (_shape, bf16)
FLAT = dict(
    x=((256, 1024), bf16),
    cot=((256, 1024), bf16),
    seg=((2, 8, 128), jnp.int32),
    gain_rows=((8, 1024), f32),
    head_gains=((8, 128), f32),
    gain_sums=((8, 1024), f32),
    head_sums=((8, 128), f32),
    mask=((2, 128, 128), f32),
    cos=((256, 128), f32),
    sin=((256, 128), f32),
    normed=((256, 1024), bf16),
    q_raw=((256, 1024), f32),
    k_raw=((256, 512), f32),
    values=((256, 512), bf16),
    q_rot=((256, 1024), bf16),
    k_rot=((256, 512), bf16),
    probs=((8, 256, 128), f32),
    attended=((256, 1024), bf16),
    out_part=((256, 1024), f32),
    out_other=((256, 1024), f32),
    hidden=((256, 1024), f32),
    mid_low=((256, 1024), bf16),
    d_mixed=((256, 1536), f32),
    mixed=((256, 1536), bf16),
    d_gate=((256, 1536), bf16),
    d_up=((256, 1536), bf16),
    down_part=((256, 1024), f32),
    down_other=((128, 1024), f32),
    mid_part=((256, 1024), f32),
    mid_other=((256, 1024), f32),
    d_res=((256, 1024), f32),
    d_res_low=((256, 1024), bf16),
    d_attn=((256, 1024), bf16),
    d_q=((256, 1024), bf16),
    d_k=((256, 512), bf16),
    d_v=((256, 512), bf16),
    in_part=((256, 1024), f32),
    in_other=((128, 1024), f32),
)
GROUPS = (W, STAGE, FIN, RX, FAR, NEAR, FLAT)
X_PAIR, COT_PAIR, SEG_PAIR, OUT_PAIR, DOWN_PAIR, MID_PAIR, IN_PAIR, FIN_PAIR = range(8)


def layer_kernel(
    tokens, segment, norm_gain, w_query, w_key, w_value, query_gain, key_gain, w_out, mlp_gain, w_gate, w_up, w_down,
    cotangent, layer_out, input_grad, out_q, out_k, out_v, out_o, out_g, out_u, out_d, out_e, *refs,
):
    refs = list(refs)
    held = []
    for group in GROUPS:
        held.append({key: refs.pop(0) for key in group})
    weight, stage, fin, rx, far_of, near_of, flat = held
    r = types.SimpleNamespace(**flat)
    gather_send, gather_recv, sum_send, sum_recv, pair_send, pair_recv, local = refs
    source = dict(q=w_query, k=w_key, v=w_value, o=w_out, g=w_gate, u=w_up, d=w_down)
    result = dict(q=out_q, k=out_k, v=out_v, o=out_o, g=out_g, u=out_u, d=out_d, e=out_e)
    pos = coords()
    me = pos["c"]
    sibling = device(pos, "c")
    own_rows = pl.ds(pl.multiple_of(me * 128, 128), 128)
    other_rows = pl.ds(pl.multiple_of((1 - me) * 128, 128), 128)

    def remote(src, dst, sems, index, target):
        return pltpu.make_async_remote_copy(
            src_ref=src, dst_ref=dst, send_sem=sems[0].at[index], recv_sem=sems[1].at[index],
            device_id=target, device_id_type=MESH,
        )

    def to_sibling(index, src, dst):
        copy = remote(src, dst, (pair_send, pair_recv), index, sibling)
        copy.start()
        return copy

    gathers = {}

    def gather_start(name, phase):
        order = ORDER[name]
        axis = order[phase]
        at = {a: pos[a] for a in order[phase:]}
        index = NAMES.index(name)
        copies = {}
        for key, half, step in ((0, 0, 1), (1, 1, -1), (2, 1, 1), (3, 0, -1)):
            src = block(weight[name], name, at, half)
            copies[key] = remote(src, src, (gather_send, gather_recv), (index, phase, key), device(pos, axis, step))
            copies[key].start()
        gathers[name, phase] = copies

    def gather_forward(name, phase):
        order = ORDER[name]
        axis = order[phase]
        at = {a: pos[a] for a in order[phase:]}
        index = NAMES.index(name)
        copies = gathers[name, phase]
        for key, got, half, step in ((4, 0, 0, 1), (5, 1, 1, -1)):
            copies[got].wait_recv()
            src = block(weight[name], name, {**at, axis: lax.rem(pos[axis] + 4 - step, 4)}, half)
            copies[key] = remote(src, src, (gather_send, gather_recv), (index, phase, key), device(pos, axis, step))
            copies[key].start()

    def gather_finish(name, phase):
        for key in (2, 3, 4, 5):
            gathers[name, phase][key].wait_recv()

    sums = {}

    def sum_start(name, phase):
        order = ORDER[name][::-1]
        axis = order[phase]
        at = {a: pos[a] for a in order[:phase]}
        ahead, behind = lax.rem(pos[axis] + 1, 4), lax.rem(pos[axis] + 3, 4)
        opposite = lax.rem(pos[axis] + 2, 4)
        up, down = device(pos, axis, 1), device(pos, axis, -1)
        index, sems = NAMES.index(name), (sum_send, sum_recv)
        cur = weight[name]
        near_up, near_down = near_of[name, phase, 0], near_of[name, phase, 1]
        copies = [
            remote(block(cur, name, {**at, axis: opposite}, 0), far_of[name, phase, 0], sems, (index, phase, 0), up),
            remote(block(cur, name, {**at, axis: opposite}, 1), far_of[name, phase, 1], sems, (index, phase, 1), down),
            remote(block(cur, name, {**at, axis: ahead}, 1), half_of(near_up, name, 1), sems, (index, phase, 2), up),
            remote(block(cur, name, {**at, axis: behind}, 0), half_of(near_down, name, 0), sems, (index, phase, 3), down),
        ]
        for copy in copies:
            copy.start()
        sums[name, phase] = copies

    def sum_middle(name, phase):
        order = ORDER[name][::-1]
        axis = order[phase]
        at = {a: pos[a] for a in order[:phase]}
        index, sems = NAMES.index(name), (sum_send, sum_recv)
        shape = halved(name, merged(name, order[: phase + 1]))
        copies = sums[name, phase]
        for half, step in ((0, 1), (1, -1)):
            far, near = far_of[name, phase, half], near_of[name, phase, half]
            copies[half].wait_recv()
            add_into(far, [far, block(weight[name], name, {**at, axis: lax.rem(pos[axis] + 4 + step, 4)}, half)], shape)
            copy = remote(far, half_of(near, name, half), sems, (index, phase, 4 + half), device(pos, axis, step))
            copy.start()
            copies.append(copy)

    def sum_end(name, phase):
        order = ORDER[name][::-1]
        at = {a: pos[a] for a in order[: phase + 1]}
        copies = sums[name, phase]
        for copy in copies[2:]:
            copy.wait_recv()
        sources = [block(weight[name], name, at), near_of[name, phase, 0], near_of[name, phase, 1]]
        if phase < 2:
            add_into(sources[0], sources, merged(name, order[: phase + 1]))
            return
        for t in range(full_shape(name)[1] if name in SPLIT else full_shape(name)[3]):
            place = (0, t, 0, 0) if name in SPLIT else (0, 0, 0, t)
            total = sources[0][place].astype(f32) + sources[1][place].astype(f32) + sources[2][place].astype(f32)
            if name in SPLIT:
                fin[name][t] = total
            else:
                result[name][8 * t : 8 * t + 8, :] = total

    spot = (pos["y"], me, pos["z"], pos["x"])
    for name in NAMES:
        kind, rows, cols, width = ARRAYS[name]
        if name == "e":
            continue
        src = source[name]
        if kind == "n":
            for b in range(cols // width):
                lanes = slice(b * width, (b + 1) * width)
                mine = src[:, lanes_at((2 * b + me) * width, width)]
                weight[name][spot + (slice(None), lanes)] = mine.astype(bf16)
                stage[name][:, lanes] = src[:, lanes_at((2 * b + 1 - me) * width, width)].astype(bf16)
        else:
            for t in range(rows // 8):
                weight[name][pos["y"], pos["z"], pos["x"], t] = src[8 * t : 8 * t + 8, :].astype(bf16)
    row_id = lax.broadcasted_iota(jnp.int32, (8, 128), 0)
    lane_id = lax.broadcasted_iota(jnp.int32, (8, 128), 1)
    gains = jnp.zeros((8, 128), f32)
    for i in range(8):
        gains = jnp.where((row_id == i) & (lane_id == 0), norm_gain[i], gains)
        gains = jnp.where((row_id == i) & (lane_id == 1), mlp_gain[i], gains)
    gains = jnp.where((row_id == 0) & (lane_id == 2), query_gain[0], gains)
    gains = jnp.where((row_id == 0) & (lane_id == 3), key_gain[0], gains).astype(bf16)
    weight["e"][spot] = gains
    stage["e"][...] = gains
    r.seg[me] = jnp.broadcast_to(segment[...], (8, 128))

    greet(pos)
    pairs = {}
    for name in ATTN + MLP:
        if name in SPLIT:
            index = FIN_PAIR + SPLIT.index(name)
            pairs[name] = to_sibling(index, stage[name], weight[name].at[spot])
    kept = []
    for i, src, dst in ((X_PAIR, tokens, r.x), (COT_PAIR, cotangent, r.cot)):
        pairs[i] = to_sibling(i, src, dst.at[own_rows])
        kept.append(pltpu.make_async_copy(src, dst.at[own_rows], local.at[i]))
        kept[i].start()
    pairs[SEG_PAIR] = to_sibling(SEG_PAIR, r.seg.at[me], r.seg.at[me])

    for name in ATTN:
        if name in pairs:
            pairs[name].wait()
        gather_start(name, 0)
    for name in MLP:
        if name in pairs:
            pairs[name].wait()
        gather_start(name, 0)
    for name in ATTN:
        gather_forward(name, 0)
    for name in ATTN:
        gather_finish(name, 0)
        gather_start(name, 1)
    for name in MLP:
        gather_forward(name, 0)
    for name in ATTN:
        gather_forward(name, 1)
    for name in ATTN:
        gather_finish(name, 1)
        gather_start(name, 2)
    for name in MLP:
        gather_finish(name, 0)
        gather_start(name, 1)

    for i in (X_PAIR, COT_PAIR, SEG_PAIR):
        pairs[i].wait()
    for copy in kept:
        copy.wait()
    freq_lane = lax.rem(lax.broadcasted_iota(jnp.int32, (128, 128), 1), 64).astype(f32)
    inv_freq = jnp.exp(freq_lane * (-2.0 / HD * LOG_THETA))
    sign = jnp.where(lax.broadcasted_iota(jnp.int32, (128, 128), 1) < 64, -1.0, 1.0)
    t_id = lax.broadcasted_iota(jnp.int32, (128, 128), 0)
    u_id = lax.broadcasted_iota(jnp.int32, (128, 128), 1)
    for b in range(2):
        ids = jnp.broadcast_to(r.seg[b, 0:1, :].astype(f32), (128, 128))
        same = ids == ids.T
        position = jnp.sum(jnp.where(same & (u_id < t_id), 1.0, 0.0), axis=1, keepdims=True)
        r.mask[b] = jnp.where(same & (u_id <= t_id), 1.0, 0.0)
        angles = position * inv_freq
        r.cos[128 * b : 128 * b + 128, :] = jnp.cos(angles)
        r.sin[128 * b : 128 * b + 128, :] = jnp.sin(angles) * sign

    for name in ATTN:
        gather_forward(name, 2)
    for name in MLP:
        gather_forward(name, 1)
    for name in MLP:
        gather_finish(name, 1)
        gather_start(name, 2)
    for name in ATTN:
        gather_finish(name, 2)

    pick = jnp.where(row_id == lane_id, 1.0, 0.0).astype(bf16)
    gain_rows = dot_nt(pick, weight["e"][...].reshape(1024, 128))
    r.gain_rows[...] = gain_rows
    eighth = lax.broadcasted_iota(jnp.int32, (1024, 128), 0) == 8 * lax.broadcasted_iota(jnp.int32, (1024, 128), 1)
    eighth = jnp.where(eighth, 1.0, 0.0).astype(bf16)
    r.head_gains[...] = dot(gain_rows.astype(bf16), eighth)
    gain_in, gain_mid = r.gain_rows.at[0:1], r.gain_rows.at[1:2]
    gain_query, gain_key = r.head_gains.at[2:3], r.head_gains.at[3:4]

    def rows_of(i, size=32):
        return pl.ds(pl.multiple_of(i * size, size), size)

    def norm_in(i):
        x = r.x[rows_of(i), :].astype(f32)
        r.normed[rows_of(i), :] = (x * inverse_rms(x) * gain_in[...]).astype(bf16)

    loop(8, norm_in)
    normed = r.normed

    def project_q(i):
        lanes = lanes_at(i * 512, 512)
        r.q_raw[:, lanes] = dot(normed[...], weight["q"][..., lanes].reshape(1024, 512))

    loop(2, project_q)
    r.k_raw[...] = dot(normed[...], weight["k"][...].reshape(1024, 512))
    r.values[...] = dot(normed[...], weight["v"][...].reshape(1024, 512)).astype(bf16)

    def rotate(vector, cos_part, sin_part):
        return vector * cos_part + pltpu.roll(vector, 64, 1) * sin_part

    def turn(src, dst, gain):
        def head(h):
            lanes = lanes_at(h * 128, 128)
            raw = src[:, lanes]
            turned = rotate(raw * inverse_rms(raw) * gain[...], r.cos[...], r.sin[...])
            dst[:, lanes] = turned.astype(bf16)

        return head

    loop(8, turn(r.q_raw, r.q_rot, gain_query))
    loop(4, turn(r.k_raw, r.k_rot, gain_key))

    def both_heads(ref, rows, m):
        first = ref[rows, lanes_at(m * 256, 128)]
        second = ref[rows, lanes_at(m * 256 + 128, 128)]
        return jnp.concatenate([first, second], axis=0)

    def attend(i):
        b, m = i // 4, lax.rem(i, 4)
        rows = pl.ds(pl.multiple_of(b * 128, 128), 128)
        lanes = lanes_at(m * 128, 128)
        scores = dot_nt(both_heads(r.q_rot, rows, m), r.k_rot[rows, lanes]) * SCALE
        mask = r.mask[b]
        masked = jnp.where(jnp.concatenate([mask, mask], axis=0) > 0.0, scores, -1e30)
        terms = jnp.exp(masked - jnp.max(masked, axis=-1, keepdims=True))
        probs = terms / jnp.sum(terms, axis=-1, keepdims=True)
        r.probs[i] = probs
        got = dot(probs.astype(bf16), r.values[rows, lanes]).astype(bf16)
        r.attended[rows, lanes_at(m * 256, 128)] = got[:128]
        r.attended[rows, lanes_at(m * 256 + 128, 128)] = got[128:]

    loop(8, attend)
    attended = r.attended

    def project_out(i):
        lanes = lanes_at(i * 512, 512)
        r.out_part[:, lanes] = dot(attended[...], weight["o"][..., lanes].reshape(1024, 512))

    loop(2, project_out)
    out_copy = to_sibling(OUT_PAIR, r.out_part, r.out_other)

    for name in MLP:
        gather_forward(name, 2)
    for name in MLP:
        gather_finish(name, 2)
    for copies in gathers.values():
        for key in range(6):
            copies[key].wait_send()

    cot = r.cot

    def mixed_back(i):
        two = weight["d"][pl.ds(2 * i, 2)].reshape(768, 1024)
        r.d_mixed[:, lanes_at(i * 768, 768)] = dot_nt(cot[...], two)

    loop(2, mixed_back)
    out_copy.wait()

    def norm_mid(i):
        rows = rows_of(i)
        hidden = r.x[rows, :].astype(f32) + (r.out_part[rows, :] + r.out_other[rows, :])
        r.hidden[rows, :] = hidden
        r.mid_low[rows, :] = (hidden * inverse_rms(hidden) * gain_mid[...]).astype(bf16)

    loop(8, norm_mid)
    mid_low = r.mid_low

    def feed(i):
        lanes = lanes_at(i * 512, 512)
        gate = dot(mid_low[...], weight["g"][..., lanes].reshape(1024, 512))
        up = dot(mid_low[...], weight["u"][..., lanes].reshape(1024, 512))
        sig = jax.nn.sigmoid(gate)
        act = gate * sig
        d_mixed = r.d_mixed[:, lanes]
        r.mixed[:, lanes] = (act * up).astype(bf16)
        r.d_gate[:, lanes] = (d_mixed * up * sig * (1.0 + gate * (1.0 - sig))).astype(bf16)
        r.d_up[:, lanes] = (d_mixed * act).astype(bf16)

    loop(3, feed)
    mixed, d_gate, d_up = r.mixed, r.d_gate, r.d_up

    def project_down(i):
        lanes = lanes_at(i * 512, 512)
        r.down_part[:, lanes] = dot(mixed[...], weight["d"][..., lanes].reshape(1536, 512))

    loop(2, project_down)
    down_copy = to_sibling(DOWN_PAIR, r.down_part.at[other_rows], r.down_other)

    def grad_down(i):
        got = dot_tn(mixed[:, lanes_at(i * 384, 384)], cot[...]).astype(bf16)
        weight["d"][i] = got.reshape(4, 4, 3, 8, 1024)

    loop(4, grad_down)
    sum_start("d", 0)

    def mid_back(i):
        got = dot_nt(d_gate[...], weight["g"][pl.ds(2 * i, 2)].reshape(512, 1536))
        got += dot_nt(d_up[...], weight["u"][pl.ds(2 * i, 2)].reshape(512, 1536))
        r.mid_part[:, lanes_at(i * 512, 512)] = got

    loop(2, mid_back)
    mid_copy = to_sibling(MID_PAIR, r.mid_part, r.mid_other)

    def grad_of(name, left, right):
        cols = ARRAYS[name][2]

        def rows(i):
            got = dot_tn(left[:, lanes_at(i * 256, 256)], right[...]).astype(bf16)
            shape = (2, 4, 4, 8, cols) if name in SPLIT else (4, 4, 2, 8, cols)
            weight[name][i] = got.reshape(shape)

        loop(4, rows)

    grad_of("g", mid_low, d_gate)
    sum_start("g", 0)
    grad_of("u", mid_low, d_up)
    sum_start("u", 0)
    mid_copy.wait()

    r.gain_sums[...] = jnp.zeros((8, 1024), f32)
    r.head_sums[...] = jnp.zeros((8, 128), f32)

    def res_back(i):
        rows = rows_of(i)
        hidden = r.hidden[rows, :]
        inverse = inverse_rms(hidden)
        unit = hidden * inverse
        part = r.mid_part[rows, :]
        r.gain_sums[1:2, :] += jnp.sum(part * unit, axis=0, keepdims=True)
        d_mid = part + r.mid_other[rows, :]
        d_res = cot[rows, :].astype(f32) + norm_backward(d_mid, unit, inverse, gain_mid[...])
        r.d_res[rows, :] = d_res
        r.d_res_low[rows, :] = d_res.astype(bf16)

    loop(8, res_back)
    d_res_low = r.d_res_low
    sum_middle("d", 0)

    def attn_back(i):
        two = weight["o"][pl.ds(2 * i, 2)].reshape(512, 1024)
        r.d_attn[:, lanes_at(i * 512, 512)] = dot_nt(d_res_low[...], two).astype(bf16)

    loop(2, attn_back)
    grad_of("o", attended, d_res_low)
    sum_start("o", 0)
    sum_middle("g", 0)
    sum_middle("u", 0)

    def head_back(grad, raw, gain):
        inverse = inverse_rms(raw)
        unit = raw * inverse
        return jnp.sum(grad * unit, axis=0, keepdims=True), norm_backward(grad, unit, inverse, gain[...])

    def attend_back(i):
        b, m = i // 4, lax.rem(i, 4)
        rows = pl.ds(pl.multiple_of(b * 128, 128), 128)
        lanes = lanes_at(m * 128, 128)
        d_att = both_heads(r.d_attn, rows, m)
        query, key = both_heads(r.q_rot, rows, m), r.k_rot[rows, lanes]
        probs = r.probs[i]
        d_probs = dot_nt(d_att, r.values[rows, lanes])
        r.d_v[rows, lanes] = dot_tn(probs.astype(bf16), d_att).astype(bf16)
        d_scores = (probs * (d_probs - jnp.sum(d_probs * probs, axis=-1, keepdims=True))).astype(bf16)
        d_query = dot(d_scores, key) * SCALE
        d_key = dot_tn(d_scores, query) * SCALE
        cos_part, sin_part = r.cos[rows, :], -r.sin[rows, :]
        for j in range(2):
            spots = lanes_at(m * 256 + 128 * j, 128)
            d_unit = rotate(d_query[128 * j : 128 * j + 128], cos_part, sin_part)
            total, d_raw = head_back(d_unit, r.q_raw[rows, spots], gain_query)
            r.head_sums[2:3, :] += total
            r.d_q[rows, spots] = d_raw.astype(bf16)
        total, d_raw = head_back(rotate(d_key, cos_part, sin_part), r.k_raw[rows, lanes], gain_key)
        r.head_sums[3:4, :] += total
        r.d_k[rows, lanes] = d_raw.astype(bf16)

    loop(8, attend_back)

    def in_back(i):
        y_pair = pl.ds(2 * i, 2)
        got = dot_nt(r.d_q[...], weight["q"][y_pair].reshape(512, 1024))
        got += dot_nt(r.d_k[...], weight["k"][y_pair].reshape(512, 512))
        got += dot_nt(r.d_v[...], weight["v"][y_pair].reshape(512, 512))
        r.in_part[:, lanes_at(i * 512, 512)] = got

    loop(2, in_back)
    in_copy = to_sibling(IN_PAIR, r.in_part.at[other_rows], r.in_other)
    grad_of("q", normed, r.d_q)
    sum_start("q", 0)
    grad_of("k", normed, r.d_k)
    sum_start("k", 0)
    grad_of("v", normed, r.d_v)
    sum_start("v", 0)

    def gain_back(i):
        x = r.x[rows_of(i), :].astype(f32)
        unit = x * inverse_rms(x)
        r.gain_sums[0:1, :] += jnp.sum(r.in_part[rows_of(i), :] * unit, axis=0, keepdims=True)

    loop(8, gain_back)
    spread = dot_nt(r.head_sums[...].astype(bf16), eighth)
    grad_e = dot_tn((r.gain_sums[...] + spread).astype(bf16), pick).astype(bf16)
    weight["e"][...] = grad_e.reshape(full_shape("e"))
    sum_start("e", 0)

    for name in MLP:
        sum_end(name, 0)
        sum_start(name, 1)
    for name in ATTN:
        sum_middle(name, 0)

    down_copy.wait()

    def finish_out(i):
        rows = rows_of(i)
        mine = pl.ds(pl.multiple_of(me * 128 + i * 32, 32), 32)
        down = r.down_part[mine, :] + r.down_other[rows, :]
        layer_out[rows, :] = (r.hidden[mine, :] + down).astype(bf16)

    loop(4, finish_out)
    in_copy.wait()

    def finish_in(i):
        rows = rows_of(i)
        mine = pl.ds(pl.multiple_of(me * 128 + i * 32, 32), 32)
        d_normed = r.in_part[mine, :] + r.in_other[rows, :]
        x = r.x[mine, :].astype(f32)
        inverse = inverse_rms(x)
        input_grad[rows, :] = r.d_res[mine, :] + norm_backward(d_normed, x * inverse, inverse, gain_in[...])

    loop(4, finish_in)

    for name in MLP:
        sum_middle(name, 1)
    for name in ATTN:
        sum_end(name, 0)
        sum_start(name, 1)
    for name in MLP:
        sum_end(name, 1)
        sum_start(name, 2)
    for name in ATTN:
        sum_middle(name, 1)
    for name in MLP:
        sum_middle(name, 2)
    for name in ATTN:
        sum_end(name, 1)
        sum_start(name, 2)
    for name in MLP:
        sum_end(name, 2)
    for name in ATTN:
        sum_middle(name, 2)
    for name in ATTN:
        sum_end(name, 2)

    last = {}
    for name in SPLIT:
        last[name] = to_sibling(FIN_PAIR + len(SPLIT) + SPLIT.index(name), fin[name].at[1 - me], rx[name])
    for name in SPLIT:
        last[name].wait()
        _, _, cols, width = ARRAYS[name]
        if name == "e":
            out_e[...] = fin["e"][me] + rx["e"][...]
            continue
        for b in range(cols // width):
            lanes = slice(b * width, (b + 1) * width)
            result[name][:, lanes_at((2 * b + me) * width, width)] = fin[name][me, :, lanes]
            result[name][:, lanes_at((2 * b + 1 - me) * width, width)] = rx[name][:, lanes]
    for copies in sums.values():
        for copy in copies:
            copy.wait_send()


def body(*args):
    vmem = pl.BlockSpec(memory_space=pltpu.VMEM)
    smem = pl.BlockSpec(memory_space=pltpu.SMEM)
    hbm = pl.BlockSpec(memory_space=pl.ANY)
    n = len(NAMES)
    shapes = [(128, 1024)] * 2 + [(8, 2048), (8, 1024), (8, 1024), (16, 1024), (8, 3072), (8, 3072), (24, 1024), (8, 128)]
    scratch = [pltpu.VMEM(*entry) for group in GROUPS for entry in group.values()]
    pair_count = FIN_PAIR + 2 * len(SPLIT)
    outs = pl.pallas_call(
        layer_kernel,
        out_shape=[jax.ShapeDtypeStruct(shape, f32 if i else bf16) for i, shape in enumerate(shapes)],
        in_specs=[hbm, vmem, smem, vmem, vmem, vmem, smem, smem, vmem, smem, vmem, vmem, vmem, hbm],
        out_specs=[vmem] * len(shapes),
        scratch_shapes=scratch
        + [pltpu.SemaphoreType.DMA((n, 3, 6))] * 4
        + [pltpu.SemaphoreType.DMA((pair_count,))] * 2
        + [pltpu.SemaphoreType.DMA((2,))],
        compiler_params=pltpu.CompilerParams(
            collective_id=1, has_side_effects=True, vmem_limit_bytes=60 << 20
        ),
        name="layer",
    )(*args)
    layer_out, input_grad, grad_q, grad_k, grad_v, grad_o, grad_g, grad_u, grad_d, gains = outs
    return (
        layer_out, input_grad, gains[:, 0], grad_q, grad_k, grad_v, gains[0, 2:3], gains[0, 3:4], grad_o, gains[:, 1],
        grad_g, grad_u, grad_d,
    )


def solution(mesh):
    rows = P(("dp", "fsdp"), None)
    flat = P(("dp", "fsdp"))
    return jax.shard_map(
        body,
        mesh=mesh,
        in_specs=(rows, rows, flat, rows, rows, rows, flat, flat, rows, flat, rows, rows, rows, rows),
        out_specs=(rows, rows, flat, rows, rows, rows, flat, flat, rows, flat, rows, rows, rows),
        check_vma=False,
    )
```

time: 3790 us -> 172 us (0.05)
  waiting for transfers between devices: 3490 us -> 0 us
  Pallas kernels: 0 us -> 159 us
  blocking collectives: 134 us -> 0 us
  matrix products: 97 us -> 0 us
    reduce_scatter x7 -> x0, waiting for transfers between devices: 3120 us -> none  [the longest x1 651 us: body(): lax.psum_scatter(grad_w_query, ('dp', 'fsdp'), scatter_dimension=0, tiled...]
    all_gather x7 -> x0, waiting for transfers between devices: 365 us -> none  [the longest x1 66 us: body(): lax.all_gather(low_mlp[1], ('dp', 'fsdp'), axis=0, tiled=True)]
    pallas_call x0 -> x1, Pallas kernels: none -> 159 us  [body(): pl.pallas_call(layer_kernel, out_shape=[jax.ShapeDtypeStruct(shape, f32 i...]
    unnamed x2 -> x0, blocking collectives: 134 us -> none
    dot_general x26 -> x0, matrix products: 93.9 us -> none  [the longest x14 60.5 us: contract(): lax.dot_general(left, right, (((left_dim,), (right_dim,)), ((), ())), pre...]
  transfers between devices with their start and end apart: 14 -> 0, of which waited for: 13 -> 0; matrix products, arithmetic and copies ran while one was open for 3% -> 0% of each run, Pallas kernels for 0% -> 0%
where the time goes in v2:
time: 172 us
  Pallas kernels  159 us (92%)
  local copies, waits for them, and re-layouts  10.5 us (6%)
  between operations  1.97 us (1%)
    pallas_call x1, Pallas kernels, body(): pl.pallas_call(layer_kernel, out_shape=[jax.ShapeDtypeStruct(shape, f32 i...  159 us
    unnamed x25, local copies, waits for them, and re-layouts  7.66 us

profile of v2, /device:TPU:1, one launch (start us, length us, event | category | flops | bytes accessed | tf_op | source)
XLA Modules:
  0.0 171.9 jit_solution(10751106228160970419)
XLA Ops:
  1.9 159.4 %layer.1 = (bf16[128,1024]{1,0:T(8,128)(2,1)}, f32[128,1024]{1,0:T(8,128)}, f32[8,2048]{1,0:T(8,128)}, f32[8,1024]{1,0:T(8,128)}, f32[8,1024]{1,0:T(8,128)}, /*i...) custom-call(bf16[128,1024]{1,0:T(8,128)(2,1)} %tokens.1, ...), custom_call_target="tpu_custom_call" | custom-call | tf_op jit(solution)/shard_map/layer/pallas_call | solution.py:727
  161.4 0.0 copy-start
  161.4 1.3 fusion
  162.7 1.5 slice_reduce_fusion
  164.2 1.7 copy.38
  165.9 0.0 copy-done
  165.9 0.0 copy-start.5
  165.9 0.8 copy.39
  166.7 0.1 copy-done.5
  166.7 0.0 copy-start.7
  166.7 0.0 copy-start.6
  166.7 0.6 copy.40
  167.4 0.1 copy-done.7
  167.5 0.0 copy-start.4
  167.5 0.6 copy.41
  168.1 0.0 copy-done.6
  168.1 0.0 copy-start.3
  168.1 0.6 copy.42
  168.7 0.0 copy-done.4
  168.7 0.6 copy.43
  169.4 0.0 copy-done.3
  169.4 0.0 copy-start.2
  169.4 0.6 copy.44
  170.0 0.3 copy-done.2
  170.3 0.0 copy-start.1
  170.3 0.6 copy.45
  170.9 0.3 copy-done.1
  171.2 0.6 copy.46
Async XLA Ops:
  161.4 4.5 %copy-start = (f32[128,1024]{1,0:T(8,128)S(1)}, f32[128,1024]{1,0:T(8,128)}, u32[]{:S(2)}) copy-start(f32[128,1024]{1,0:T(8,128)} %get-tuple-element.51) | copy-start | bytes 1572868
  165.9 0.9 copy-start.5
  166.7 0.8 copy-start.7
  166.7 1.4 copy-start.6
  167.5 1.2 copy-start.4
  168.1 1.3 copy-start.3
  169.4 0.9 copy-start.2
  170.3 0.9 copy-start.1

commit v3 on v2

v3 whole, which is shorter than its diff:
```python
import types

import jax
import jax.numpy as jnp
from jax import lax
from jax.experimental import pallas as pl
from jax.experimental.pallas import tpu as pltpu
from jax.sharding import PartitionSpec as P

HD = 128
EPS = 1e-06
LOG_THETA = 13.815510557964274
SCALE = HD ** (-0.5)

bf16 = jnp.bfloat16
f32 = jnp.float32
MESH = pl.DeviceIdType.MESH

SHAPES = dict(
    q=(4, 2, 4, 4, 8, 1024),
    b=(4, 2, 4, 4, 8, 1024),
    o=(4, 4, 4, 2, 8, 1024),
    e=(4, 2, 4, 4, 1, 128),
    g=(3, 4, 2, 4, 4, 8, 512),
    u=(3, 4, 2, 4, 4, 8, 512),
    d=(3, 4, 4, 4, 8, 1024),
)
NAMES = tuple(SHAPES)
SPLIT = ("q", "b", "e", "g", "u")
ATTN = ("q", "b", "o")
MLP = ("g", "u", "d")
ORDER = dict(q="xyz", g="xyz", b="yzx", u="yzx", o="zxy", d="zxy", e="zxy")
DTYPE = {name: f32 if name == "e" else bf16 for name in NAMES}


def coords():
    dp = lax.axis_index("dp")
    fs = lax.axis_index("fsdp")
    return dict(y=dp // 2, c=lax.rem(dp, 2), z=fs // 4, x=lax.rem(fs, 4))


def device(pos, axis=None, step=0):
    pos = dict(pos)
    if axis == "c":
        pos["c"] = 1 - pos["c"]
    elif axis is not None:
        pos[axis] = lax.rem(pos[axis] + step + 4, 4)
    return (pos["y"] * 2 + pos["c"], pos["z"] * 4 + pos["x"])


def item_shape(item):
    name, third = item
    return SHAPES[name] if third is None else SHAPES[name][1:]


def lead_of(item):
    return 1 if item[0] in MLP and item[1] is None else 0


def axis_places(item):
    lead = lead_of(item)
    if item[0] in SPLIT:
        return dict(y=lead, z=lead + 2, x=lead + 3)
    return dict(y=lead, z=lead + 1, x=lead + 2)


def block(ref, item, at, half=None):
    shape = item_shape(item)
    index = [slice(None)] * len(shape)
    for axis, place in axis_places(item).items():
        if axis in at:
            start, size = at[axis] if isinstance(at[axis], tuple) else (at[axis], 1)
            index[place] = pl.ds(start, size)
    if half is not None:
        if item[0] in SPLIT:
            index[lead_of(item) + 1] = pl.ds(half, 1)
        else:
            index[-1] = pl.ds(half * (shape[-1] // 2), shape[-1] // 2)
    return ref.at[tuple(index)]


def half_of(ref, item, half):
    return block(ref, item, {}, half)


def merged(item, fixed):
    shape = list(item_shape(item))
    for axis in fixed:
        shape[axis_places(item)[axis]] = 1
    return tuple(shape)


def halved(item, shape):
    shape = list(shape)
    shape[lead_of(item) + 1 if item[0] in SPLIT else -1] //= 2
    return tuple(shape)


def add_into(dst, sources, shape):
    lead = shape[:-3]
    count = 1
    for extent in lead:
        count *= extent

    def step(i, carry):
        index, rest = [], i
        for extent in reversed(lead):
            index.append(lax.rem(rest, extent))
            rest = rest // extent
        index = tuple(reversed(index))
        total = sources[0][index].astype(f32)
        for source in sources[1:]:
            total = total + source[index].astype(f32)
        dst[index] = total.astype(dst.dtype)
        return carry

    lax.fori_loop(0, count, step, 0)


def dot(left, right):
    return jnp.dot(left, right, preferred_element_type=f32)


def dot_nt(left, right):
    return lax.dot_general(left, right, (((1,), (1,)), ((), ())), preferred_element_type=f32)


def dot_tn(left, right):
    return lax.dot_general(left, right, (((0,), (0,)), ((), ())), preferred_element_type=f32)


def inverse_rms(vector):
    return lax.rsqrt(jnp.mean(vector * vector, axis=-1, keepdims=True) + EPS)


def norm_backward(grad_in, unit_vec, inverse, gain_vec):
    scaled = grad_in * gain_vec
    return inverse * (scaled - unit_vec * jnp.mean(scaled * unit_vec, axis=-1, keepdims=True))


def lanes_at(start, size):
    return pl.ds(pl.multiple_of(start, 128), size)


def rows_at(start, size):
    return pl.ds(pl.multiple_of(start, 8), size)


def loop(count, body):
    def step(i, carry):
        body(i)
        return carry

    lax.fori_loop(0, count, step, 0)


ALL = (("q", None), ("b", None), ("o", None), ("e", None), ("g", None), ("u", None), ("d", None))
THIRDS = tuple((name, t) for t in range(3) for name in MLP)
ITEMS = ALL + THIRDS
SUMS = tuple((item, phase) for item in ALL for phase in range(3) if item[0] not in MLP or phase > 0)
SUMS += tuple((item, 0) for item in THIRDS)


def is_direct(item, phase):
    return phase == 2 or item[0] == "e" or (phase == 1 and item[0] not in MLP)


GATHERS = tuple((item, phase) for item in ALL for phase in range(3) if item[0] not in MLP or phase < 2)
GATHERS += tuple((item, 2) for item in THIRDS)
SEMS = {}
for _kind, _steps in enumerate((GATHERS, SUMS)):
    for _item, _phase in _steps:
        _direct = is_direct(_item, _phase) if _kind else _phase == 0 or _item[0] == "e"
        for _use in range(2 if _direct else 3):
            SEMS[_kind, _item, _phase, _use] = len(SEMS)
W = {name: (SHAPES[name], DTYPE[name]) for name in NAMES}
STAGE = dict(q=((8, 1024), bf16), b=((8, 1024), bf16), e=((1, 128), f32), g=((3, 8, 512), bf16), u=((3, 8, 512), bf16))
FIN = dict(q=((2, 8, 1024), f32), b=((2, 8, 1024), f32), e=((2, 1, 128), f32), g=((2, 3, 8, 512), f32), u=((2, 3, 8, 512), f32))
RX = dict(q=((8, 1024), f32), b=((8, 1024), f32), e=((1, 128), f32), g=((3, 8, 512), f32), u=((3, 8, 512), f32))
FAR, NEAR = {}, {}
for _item, _phase in SUMS:
    _shape = merged(_item, ORDER[_item[0]][::-1][: _phase + 1])
    for _way in range(2):
        NEAR[_item, _phase, _way] = (_shape, DTYPE[_item[0]])
        if not is_direct(_item, _phase):
            FAR[_item, _phase, _way] = (halved(_item, _shape), DTYPE[_item[0]])
    if is_direct(_item, _phase):
        FAR[_item, _phase, 2] = (_shape, DTYPE[_item[0]])
INS = (
    ((8, 2048), f32), ((8, 1024), f32), ((8, 1024), f32), ((16, 1024), f32), ((8, 3072), f32), ((8, 3072), f32), ((24, 1024), f32),
)
OUTS = (((128, 1024), bf16), ((128, 1024), f32)) + INS + (((8, 128), f32),)
IN_BUF = {i: entry for i, entry in enumerate(INS)}
OUT_BUF = {i: entry for i, entry in enumerate(OUTS)}
FLAT = dict(
    x=((256, 1024), bf16),
    cot=((256, 1024), bf16),
    seg=((2, 8, 128), jnp.int32),
    perm=((384, 384), bf16),
    blocks=((128, 384), f32),
    eighths=((2, 1024, 128), bf16),
    gain_rows=((8, 1024), f32),
    head_gains=((8, 128), f32),
    gain_sums=((8, 1024), f32),
    head_sums=((8, 128), f32),
    mask=((2, 128, 128), f32),
    cos=((256, 128), f32),
    sin=((256, 128), f32),
    normed=((256, 1024), bf16),
    q_raw=((256, 1024), f32),
    k_raw=((256, 512), f32),
    values=((256, 512), bf16),
    q_rot=((256, 1024), bf16),
    k_rot=((256, 512), bf16),
    probs=((8, 256, 128), f32),
    attended=((256, 1024), bf16),
    out_part=((256, 1024), f32),
    out_other=((256, 1024), f32),
    hidden=((256, 1024), f32),
    mid_low=((256, 1024), bf16),
    mixed=((256, 512), bf16),
    d_gate=((256, 512), bf16),
    d_up=((256, 512), bf16),
    down_part=((256, 1024), f32),
    down_other=((128, 1024), f32),
    mid_part=((256, 1024), f32),
    mid_other=((256, 1024), f32),
    d_res=((256, 1024), f32),
    d_res_low=((256, 1024), bf16),
    d_attn=((256, 1024), bf16),
    d_q=((256, 1024), bf16),
    d_b=((256, 1024), bf16),
    in_part=((256, 1024), f32),
    in_other=((128, 1024), f32),
)
GROUPS = (W, STAGE, FIN, RX, FAR, NEAR, IN_BUF, OUT_BUF, FLAT)
X_PAIR, COT_PAIR, SEG_PAIR, OUT_PAIR, DOWN_PAIR, MID_PAIR, IN_PAIR, STAGE_PAIR = range(8)
FIN_PAIR = STAGE_PAIR + len(SPLIT)
PAIRS = FIN_PAIR + len(SPLIT)


def layer_kernel(
    tokens, segment, norm_gain, w_query, w_key, w_value, query_gain, key_gain, w_out, mlp_gain, w_gate, w_up, w_down,
    cotangent, *refs,
):
    refs = list(refs)
    outputs = [refs.pop(0) for _ in OUTS]
    held = []
    for group in GROUPS:
        held.append({key: refs.pop(0) for key in group})
    weight, stage, fin, rx, far_of, near_of, in_buf, out_buf, flat = held
    r = types.SimpleNamespace(**flat)
    sems, pair_send, pair_recv, local_in, local_out = refs
    pos = coords()
    me = pos["c"]
    sibling = device(pos, "c")
    own_rows = pl.ds(pl.multiple_of(me * 128, 128), 128)
    other_rows = pl.ds(pl.multiple_of((1 - me) * 128, 128), 128)
    layer_out, input_grad = out_buf[0], out_buf[1]

    barrier = pltpu.get_barrier_semaphore()
    others = [sibling]
    for axis in "xyz":
        others += [device(pos, axis, step) for step in (1, -1, 2)]
    for other in others:
        pl.semaphore_signal(barrier, inc=1, device_id=other, device_id_type=MESH)
    fetches = []
    for i, src in enumerate((w_query, w_key, w_value, w_out, w_gate, w_up, w_down)):
        fetches.append(pltpu.make_async_copy(src, in_buf[i], local_in.at[i]))
    fetches.append(pltpu.make_async_copy(tokens, r.x.at[own_rows], local_in.at[7]))
    fetches.append(pltpu.make_async_copy(cotangent, r.cot.at[own_rows], local_in.at[8]))
    for copy in fetches:
        copy.start()

    def remote(src, dst, send_sem, recv_sem, target):
        return pltpu.make_async_remote_copy(
            src_ref=src, dst_ref=dst, send_sem=send_sem, recv_sem=recv_sem, device_id=target, device_id_type=MESH
        )

    def to_sibling(index, src, dst):
        copy = remote(src, dst, pair_send.at[index], pair_recv.at[index], sibling)
        copy.start()
        return copy

    def sem(kind, item, phase, use):
        return sems.at[SEMS[kind, item, phase, use]]

    def send(kind, item, phase, use, src, dst, target):
        remote(src, dst, sem(kind, item, phase, 0), sem(kind, item, phase, use), target).start()

    def wait_for(kind, item, phase, use, count):
        order = ORDER[item[0]] if kind == 0 else ORDER[item[0]][::-1]
        fixed = order[phase + 1 :] if kind == 0 else order[:phase]
        like = block(view(item), item, {**{a: pos[a] for a in fixed}, order[phase]: (0, count)})
        pltpu.make_async_copy(like, like, sem(kind, item, phase, use)).wait()

    def view(item):
        name, third = item
        return weight[name] if third is None else weight[name].at[third]

    def gather_start(item, phase, keys=(0, 1, 2, 3)):
        order = ORDER[item[0]]
        axis = order[phase]
        at = {a: pos[a] for a in order[phase:]}
        if phase == 0 or item[0] == "e":
            for step in (1, -1, 2):
                src = block(view(item), item, at)
                send(0, item, phase, 1, src, src, device(pos, axis, step))
            return
        for key, half, step in ((0, 0, 1), (1, 1, -1), (2, 1, 1), (3, 0, -1)):
            if key in keys:
                src = block(view(item), item, at, half)
                send(0, item, phase, 1 if key < 2 else 2, src, src, device(pos, axis, step))

    def gather_forward(item, phase):
        order = ORDER[item[0]]
        axis = order[phase]
        at = {a: pos[a] for a in order[phase:]}
        wait_for(0, item, phase, 1, 1)
        for half, step in ((0, 1), (1, -1)):
            src = block(view(item), item, {**at, axis: lax.rem(pos[axis] + 4 - step, 4)}, half)
            send(0, item, phase, 2, src, src, device(pos, axis, step))

    def gather_finish(item, phase):
        if phase == 0 or item[0] == "e":
            wait_for(0, item, phase, 1, 3)
        else:
            wait_for(0, item, phase, 2, 2)

    def sum_start(item, phase):
        order = ORDER[item[0]][::-1]
        axis = order[phase]
        at = {a: pos[a] for a in order[:phase]}
        ahead, behind = lax.rem(pos[axis] + 1, 4), lax.rem(pos[axis] + 3, 4)
        opposite = lax.rem(pos[axis] + 2, 4)
        up, down, across = device(pos, axis, 1), device(pos, axis, -1), device(pos, axis, 2)
        cur = view(item)
        near_up, near_down = near_of[item, phase, 0], near_of[item, phase, 1]

        def part(place, half=None):
            return block(cur, item, {**at, axis: place}, half)

        if is_direct(item, phase):
            send(1, item, phase, 1, part(opposite), far_of[item, phase, 2], across)
            send(1, item, phase, 1, part(ahead), near_up, up)
            send(1, item, phase, 1, part(behind), near_down, down)
        else:
            send(1, item, phase, 1, part(opposite, 0), far_of[item, phase, 0], up)
            send(1, item, phase, 1, part(opposite, 1), far_of[item, phase, 1], down)
            send(1, item, phase, 2, part(ahead, 1), half_of(near_up, item, 1), up)
            send(1, item, phase, 2, part(behind, 0), half_of(near_down, item, 0), down)

    def sum_middle(item, phase):
        order = ORDER[item[0]][::-1]
        axis = order[phase]
        at = {a: pos[a] for a in order[:phase]}
        shape = halved(item, merged(item, order[: phase + 1]))
        wait_for(1, item, phase, 1, 1)
        for half, step in ((0, 1), (1, -1)):
            far, near = far_of[item, phase, half], near_of[item, phase, half]
            mine = block(view(item), item, {**at, axis: lax.rem(pos[axis] + 4 + step, 4)}, half)
            add_into(far, [far, mine], shape)
            send(1, item, phase, 2, far, half_of(near, item, half), device(pos, axis, step))

    def sum_end(item, phase):
        order = ORDER[item[0]][::-1]
        at = {a: pos[a] for a in order[: phase + 1]}
        sources = [block(view(item), item, at), near_of[item, phase, 0], near_of[item, phase, 1]]
        if is_direct(item, phase):
            sources.append(far_of[item, phase, 2])
            wait_for(1, item, phase, 1, 3)
        else:
            wait_for(1, item, phase, 2, 2)
        if phase < 2:
            add_into(sources[0], sources, merged(item, order[: phase + 1]))
            return

        def total(place):
            value = sources[0][place].astype(f32)
            for source in sources[1:]:
                value = value + source[place].astype(f32)
            return value

        name = item[0]
        if name in MLP:
            for t in range(3):
                if name == "d":
                    out_buf[8][8 * t : 8 * t + 8, :] = total((t, 0, 0, 0))
                else:
                    for c in range(2):
                        fin[name][c, t] = total((t, 0, c, 0, 0))
        elif name == "o":
            for t in range(2):
                out_buf[5][8 * t : 8 * t + 8, :] = total((0, 0, 0, t))
        else:
            for c in range(2):
                fin[name][c] = total((0, c, 0, 0))

    spot = (pos["y"], me, pos["z"], pos["x"])

    def stage_columns(name, buf, start, count, width, place):
        for i in range(count):
            lanes = slice(place + i * width, place + (i + 1) * width)
            weight[name][spot + (slice(None), lanes)] = in_buf[buf][:, lanes_at((2 * i + me) * width, width)].astype(bf16)
            stage[name][:, lanes] = in_buf[buf][:, lanes_at((2 * i + 1 - me) * width, width)].astype(bf16)

    row_id = lax.broadcasted_iota(jnp.int32, (8, 128), 0)
    lane_id = lax.broadcasted_iota(jnp.int32, (8, 128), 1)
    lane_row = lax.broadcasted_iota(jnp.int32, (1, 128), 1)
    gains = jnp.zeros((1, 128), f32)
    for i in range(8):
        gains = jnp.where(lane_row == i, norm_gain[i], gains)
        gains = jnp.where(lane_row == 8 + i, mlp_gain[i], gains)
    gains = jnp.where(lane_row == 16, query_gain[0], gains)
    gains = jnp.where(lane_row == 17, key_gain[0], gains).astype(bf16).astype(f32)
    weight["e"][spot] = gains
    stage["e"][...] = gains
    r.seg[me] = jnp.broadcast_to(segment[...], (8, 128))
    for i in range(4):
        fetches[i].wait()
    stage_columns("q", 0, 0, 4, 256, 0)
    stage_columns("b", 1, 0, 4, 128, 0)
    stage_columns("b", 2, 0, 4, 128, 512)
    for t in range(2):
        weight["o"][pos["y"], pos["z"], pos["x"], t] = in_buf[3][8 * t : 8 * t + 8, :].astype(bf16)

    pl.semaphore_wait(barrier, len(others))
    pairs = {}

    def pair_start(name):
        index = STAGE_PAIR + SPLIT.index(name)
        if name in MLP:
            dst = weight[name].at[:, pos["y"], me, pos["z"], pos["x"]]
        else:
            dst = weight[name].at[spot]
        pairs[name] = to_sibling(index, stage[name], dst)

    for name in ("q", "b", "e"):
        pair_start(name)

    to_lane = lax.broadcasted_iota(jnp.int32, (384, 384), 1)
    from_lane = ((to_lane >> 3) & 15) * 24 + (to_lane >> 7) * 8 + (to_lane & 7)
    r.perm[...] = jnp.where(lax.broadcasted_iota(jnp.int32, (384, 384), 0) == from_lane, 1.0, 0.0).astype(bf16)
    for i in range(4, 7):
        fetches[i].wait()
    for i, buf in ((0, 4), (1, 5)):
        for b in range(8):
            r.blocks[64 * i + 8 * b : 64 * i + 8 * b + 8, :] = in_buf[buf][:, 384 * b : 384 * b + 384]
    r.blocks[...] = dot(r.blocks[...].astype(bf16), r.perm[...])
    for i, name in ((0, "g"), (1, "u")):
        for y in range(4):
            mine = r.blocks[rows_at(64 * i + 8 * (2 * y + me), 8), :].astype(bf16)
            theirs = r.blocks[rows_at(64 * i + 8 * (2 * y + 1 - me), 8), :].astype(bf16)
            for t in range(3):
                lanes = slice(128 * y, 128 * y + 128)
                weight[name][(t,) + spot + (slice(None), lanes)] = mine[:, 128 * t : 128 * t + 128]
                stage[name][t, :, lanes] = theirs[:, 128 * t : 128 * t + 128]
    for t in range(3):
        weight["d"][t, pos["y"], pos["z"], pos["x"]] = in_buf[6][8 * t : 8 * t + 8, :].astype(bf16)
    for name in ("g", "u"):
        pair_start(name)
    for name in ("e", "q", "b"):
        pairs[name].wait()
    for name in ("e", "q", "b", "o"):
        gather_start((name, None), 0)
    for name in ("g", "u"):
        pairs[name].wait()
    for name in MLP:
        gather_start((name, None), 0)
    fetches[7].wait()
    fetches[8].wait()
    pairs[X_PAIR] = to_sibling(X_PAIR, r.x.at[own_rows], r.x.at[own_rows])
    pairs[SEG_PAIR] = to_sibling(SEG_PAIR, r.seg.at[me], r.seg.at[me])
    pairs[COT_PAIR] = to_sibling(COT_PAIR, r.cot.at[own_rows], r.cot.at[own_rows])
    for name in ("e",) + ATTN:
        gather_finish((name, None), 0)
        gather_start((name, None), 1)
    for name in MLP:
        gather_finish((name, None), 0)
        gather_start((name, None), 1, (0, 1))

    for i in (X_PAIR, SEG_PAIR, COT_PAIR):
        pairs[i].wait()
    freq_lane = lax.rem(lax.broadcasted_iota(jnp.int32, (128, 128), 1), 64).astype(f32)
    inv_freq = jnp.exp(freq_lane * (-2.0 / HD * LOG_THETA))
    sign = jnp.where(lax.broadcasted_iota(jnp.int32, (128, 128), 1) < 64, -1.0, 1.0)
    t_id = lax.broadcasted_iota(jnp.int32, (128, 128), 0)
    u_id = lax.broadcasted_iota(jnp.int32, (128, 128), 1)

    def angles_of(b):
        ids = jnp.broadcast_to(r.seg[b, 0:1, :].astype(f32), (128, 128))
        same = ids == ids.T
        position = jnp.sum(jnp.where(same & (u_id < t_id), 1.0, 0.0), axis=1, keepdims=True)
        r.mask[b] = jnp.where(same & (u_id <= t_id), 1.0, 0.0)
        angles = position * inv_freq
        r.cos[128 * b : 128 * b + 128, :] = jnp.cos(angles)
        r.sin[128 * b : 128 * b + 128, :] = jnp.sin(angles) * sign

    angles_of(0)
    for name in ATTN:
        gather_forward((name, None), 1)
    for name in MLP:
        gather_start((name, None), 1, (2, 3))
    angles_of(1)
    gather_finish(("e", None), 1)
    gather_start(("e", None), 2)
    for name in ATTN:
        gather_finish((name, None), 1)
        gather_start((name, None), 2)
    for name in MLP:
        gather_forward((name, None), 1)

    unit_lane = lax.broadcasted_iota(jnp.int32, (1024, 128), 1)
    unit_row = lax.broadcasted_iota(jnp.int32, (1024, 128), 0) & 7
    r.eighths[0] = jnp.where(unit_lane == unit_row, 1.0, 0.0).astype(bf16)
    r.eighths[1] = jnp.where(unit_lane == unit_row + 8, 1.0, 0.0).astype(bf16)
    owner = lax.broadcasted_iota(jnp.int32, (128, 1024), 1) >> 3
    owned = owner == lax.broadcasted_iota(jnp.int32, (128, 1024), 0)
    pick = ((row_id == 2) & (lane_id == 16)) | ((row_id == 3) & (lane_id == 17))
    pick = jnp.where(pick, 1.0, 0.0).astype(bf16)
    gather_finish(("e", None), 2)
    table = weight["e"][...].reshape(128, 128).astype(bf16)
    for i in range(2):
        spread = jnp.where(owned, dot_nt(table, r.eighths[i]), 0.0)
        r.gain_rows[i : i + 1, :] = jnp.sum(spread, axis=0, keepdims=True)
    r.head_gains[...] = dot_nt(pick, table)
    gain_in, gain_mid = r.gain_rows.at[0:1], r.gain_rows.at[1:2]
    gain_query, gain_key = r.head_gains.at[2:3], r.head_gains.at[3:4]

    def rows_of(i, size=32):
        return pl.ds(pl.multiple_of(i * size, size), size)

    def norm_in(i):
        x = r.x[rows_of(i), :].astype(f32)
        r.normed[rows_of(i), :] = (x * inverse_rms(x) * gain_in[...]).astype(bf16)

    loop(8, norm_in)
    normed, cot = r.normed, r.cot
    for name in MLP:
        gather_finish((name, None), 1)
    for name in ATTN:
        gather_forward((name, None), 2)
    for name in MLP:
        gather_start((name, 0), 2)
    for name in MLP:
        gather_start((name, 1), 2, (0, 1))
    for name in ATTN:
        gather_finish((name, None), 2)

    def project_q(i):
        lanes = lanes_at(i * 512, 512)
        r.q_raw[:, lanes] = dot(normed[...], weight["q"][..., lanes].reshape(1024, 512))

    loop(2, project_q)
    r.k_raw[...] = dot(normed[...], weight["b"][..., :512].reshape(1024, 512))
    r.values[...] = dot(normed[...], weight["b"][..., 512:].reshape(1024, 512)).astype(bf16)

    def rotate(vector, cos_part, sin_part):
        return vector * cos_part + pltpu.roll(vector, 64, 1) * sin_part

    def turn(src, dst, gain):
        def head(h):
            lanes = lanes_at(h * 128, 128)
            raw = src[:, lanes]
            turned = rotate(raw * inverse_rms(raw) * gain[...], r.cos[...], r.sin[...])
            dst[:, lanes] = turned.astype(bf16)

        return head

    loop(8, turn(r.q_raw, r.q_rot, gain_query))
    loop(4, turn(r.k_raw, r.k_rot, gain_key))

    for name in MLP:
        gather_forward((name, 0), 2)
    for name in MLP:
        gather_start((name, 1), 2, (2, 3))
    for name in MLP:
        gather_start((name, 2), 2, (0, 1))

    def both_heads(ref, rows, m):
        first = ref[rows, lanes_at(m * 256, 128)]
        second = ref[rows, lanes_at(m * 256 + 128, 128)]
        return jnp.concatenate([first, second], axis=0)

    def attend(i):
        b, m = i // 4, lax.rem(i, 4)
        rows = pl.ds(pl.multiple_of(b * 128, 128), 128)
        lanes = lanes_at(m * 128, 128)
        scores = dot_nt(both_heads(r.q_rot, rows, m), r.k_rot[rows, lanes]) * SCALE
        mask = r.mask[b]
        masked = jnp.where(jnp.concatenate([mask, mask], axis=0) > 0.0, scores, -1e30)
        terms = jnp.exp(masked - jnp.max(masked, axis=-1, keepdims=True))
        probs = terms / jnp.sum(terms, axis=-1, keepdims=True)
        r.probs[i] = probs
        got = dot(probs.astype(bf16), r.values[rows, lanes]).astype(bf16)
        r.attended[rows, lanes_at(m * 256, 128)] = got[:128]
        r.attended[rows, lanes_at(m * 256 + 128, 128)] = got[128:]

    loop(8, attend)
    attended = r.attended

    def project_out(i):
        lanes = lanes_at(i * 512, 512)
        r.out_part[:, lanes] = dot(attended[...], weight["o"][..., lanes].reshape(1024, 512))

    loop(2, project_out)
    out_copy = to_sibling(OUT_PAIR, r.out_part, r.out_other)
    for name in MLP:
        gather_forward((name, 1), 2)
    for name in MLP:
        gather_start((name, 2), 2, (2, 3))
    out_copy.wait()

    def norm_mid(i):
        rows = rows_of(i)
        hidden = r.x[rows, :].astype(f32) + (r.out_part[rows, :] + r.out_other[rows, :])
        r.hidden[rows, :] = hidden
        r.mid_low[rows, :] = (hidden * inverse_rms(hidden) * gain_mid[...]).astype(bf16)

    loop(8, norm_mid)
    mid_low, mixed, d_gate, d_up = r.mid_low, r.mixed, r.d_gate, r.d_up

    def feed(t):
        gate = dot(mid_low[...], weight["g"][t].reshape(1024, 512))
        up = dot(mid_low[...], weight["u"][t].reshape(1024, 512))
        d_mixed = dot_nt(cot[...], weight["d"][t].reshape(512, 1024))
        sig = jax.nn.sigmoid(gate)
        act = gate * sig
        mixed[...] = (act * up).astype(bf16)
        d_gate[...] = (d_mixed * up * sig * (1.0 + gate * (1.0 - sig))).astype(bf16)
        d_up[...] = (d_mixed * act).astype(bf16)

        def mid_back(i):
            y_pair, lanes = pl.ds(2 * i, 2), lanes_at(i * 512, 512)
            got = dot_nt(d_gate[...], weight["g"][t, y_pair].reshape(512, 512))
            got += dot_nt(d_up[...], weight["u"][t, y_pair].reshape(512, 512))
            r.mid_part[:, lanes] = got if t == 0 else r.mid_part[:, lanes] + got

        def project_down(i):
            lanes = lanes_at(i * 512, 512)
            got = dot(mixed[...], weight["d"][t, ..., lanes].reshape(512, 512))
            r.down_part[:, lanes] = got if t == 0 else r.down_part[:, lanes] + got

        loop(2, mid_back)
        if t == 2:
            pairs[MID_PAIR] = to_sibling(MID_PAIR, r.mid_part, r.mid_other)
        loop(2, project_down)

    def grads(t):
        def grad_down(i):
            got = dot_tn(mixed[:, lanes_at(i * 256, 256)], cot[...]).astype(bf16)
            weight["d"][t, pl.ds(2 * i, 2)] = got.reshape(2, 4, 4, 8, 1024)

        def grad_gate(i):
            left = mid_low[:, lanes_at(i * 512, 512)]
            weight["g"][t, pl.ds(2 * i, 2)] = dot_tn(left, d_gate[...]).astype(bf16).reshape(2, 2, 4, 4, 8, 512)
            weight["u"][t, pl.ds(2 * i, 2)] = dot_tn(left, d_up[...]).astype(bf16).reshape(2, 2, 4, 4, 8, 512)

        loop(2, grad_down)
        loop(2, grad_gate)

    def sends_done(item, phases):
        for phase in phases:
            wait_for(0, item, phase, 0, 3)

    for name in MLP:
        gather_finish((name, 0), 2)
    feed(0)
    for name in MLP:
        gather_forward((name, 2), 2)
    for name in MLP:
        sends_done((name, None), (0, 1))
        sends_done((name, 0), (2,))
    grads(0)
    for name in MLP:
        sum_start((name, 0), 0)
    for name in MLP:
        gather_finish((name, 1), 2)
    feed(1)
    for name in MLP:
        sends_done((name, 1), (2,))
    grads(1)
    for name in MLP:
        sum_start((name, 1), 0)
    for name in MLP:
        gather_finish((name, 2), 2)
    feed(2)
    for name in MLP:
        sends_done((name, 2), (2,))
    grads(2)
    for name in MLP:
        sum_start((name, 2), 0)
    down_copy = to_sibling(DOWN_PAIR, r.down_part.at[other_rows], r.down_other)
    for name in MLP:
        sum_middle((name, 0), 0)
    pairs[MID_PAIR].wait()

    r.gain_sums[...] = jnp.zeros((8, 1024), f32)
    r.head_sums[...] = jnp.zeros((8, 128), f32)

    def res_back(i):
        rows = rows_of(i)
        hidden = r.hidden[rows, :]
        inverse = inverse_rms(hidden)
        unit = hidden * inverse
        part = r.mid_part[rows, :]
        r.gain_sums[1:2, :] += jnp.sum(part * unit, axis=0, keepdims=True)
        d_mid = part + r.mid_other[rows, :]
        d_res = cot[rows, :].astype(f32) + norm_backward(d_mid, unit, inverse, gain_mid[...])
        r.d_res[rows, :] = d_res
        r.d_res_low[rows, :] = d_res.astype(bf16)

    loop(8, res_back)
    d_res_low = r.d_res_low

    def attn_back(i):
        two = weight["o"][pl.ds(2 * i, 2)].reshape(512, 1024)
        r.d_attn[:, lanes_at(i * 512, 512)] = dot_nt(d_res_low[...], two).astype(bf16)

    loop(2, attn_back)
    for name in ATTN + ("e",):
        sends_done((name, None), (0, 1, 2))

    def grad_of(name, left, right):
        def rows(i):
            got = dot_tn(left[:, lanes_at(i * 512, 512)], right[...]).astype(bf16)
            weight[name][pl.ds(2 * i, 2)] = got.reshape((2,) + SHAPES[name][1:])

        loop(2, rows)

    grad_of("o", attended, d_res_low)
    sum_start(("o", None), 0)
    for name in MLP:
        sum_middle((name, 1), 0)

    def head_back(grad, raw, gain):
        inverse = inverse_rms(raw)
        unit = raw * inverse
        return jnp.sum(grad * unit, axis=0, keepdims=True), norm_backward(grad, unit, inverse, gain[...])

    def attend_back(i):
        b, m = i // 4, lax.rem(i, 4)
        rows = pl.ds(pl.multiple_of(b * 128, 128), 128)
        lanes = lanes_at(m * 128, 128)
        d_att = both_heads(r.d_attn, rows, m)
        query, key = both_heads(r.q_rot, rows, m), r.k_rot[rows, lanes]
        probs = r.probs[i]
        d_probs = dot_nt(d_att, r.values[rows, lanes])
        r.d_b[rows, lanes_at(512 + m * 128, 128)] = dot_tn(probs.astype(bf16), d_att).astype(bf16)
        d_scores = (probs * (d_probs - jnp.sum(d_probs * probs, axis=-1, keepdims=True))).astype(bf16)
        d_query = dot(d_scores, key) * SCALE
        d_key = dot_tn(d_scores, query) * SCALE
        cos_part, sin_part = r.cos[rows, :], -r.sin[rows, :]
        for j in range(2):
            spots = lanes_at(m * 256 + 128 * j, 128)
            d_unit = rotate(d_query[128 * j : 128 * j + 128], cos_part, sin_part)
            total, d_raw = head_back(d_unit, r.q_raw[rows, spots], gain_query)
            r.head_sums[2:3, :] += total
            r.d_q[rows, spots] = d_raw.astype(bf16)
        total, d_raw = head_back(rotate(d_key, cos_part, sin_part), r.k_raw[rows, lanes], gain_key)
        r.head_sums[3:4, :] += total
        r.d_b[rows, lanes] = d_raw.astype(bf16)

    loop(8, attend_back)
    for name in MLP:
        sum_middle((name, 2), 0)

    def in_back(i):
        y_pair = pl.ds(2 * i, 2)
        got = dot_nt(r.d_q[...], weight["q"][y_pair].reshape(512, 1024))
        got += dot_nt(r.d_b[...], weight["b"][y_pair].reshape(512, 1024))
        r.in_part[:, lanes_at(i * 512, 512)] = got

    loop(2, in_back)
    in_copy = to_sibling(IN_PAIR, r.in_part.at[other_rows], r.in_other)
    grad_of("q", normed, r.d_q)
    sum_start(("q", None), 0)
    grad_of("b", normed, r.d_b)
    sum_start(("b", None), 0)

    for t in range(3):
        for name in MLP:
            sum_end((name, t), 0)
    for name in MLP:
        sum_start((name, None), 1)

    def gain_back(i):
        x = r.x[rows_of(i), :].astype(f32)
        unit = x * inverse_rms(x)
        r.gain_sums[0:1, :] += jnp.sum(r.in_part[rows_of(i), :] * unit, axis=0, keepdims=True)

    loop(8, gain_back)
    table = dot_tn(r.head_sums[...].astype(bf16), pick)
    for i in range(2):
        table += dot(jnp.where(owned, r.gain_sums[i : i + 1, :], 0.0).astype(bf16), r.eighths[i])
    weight["e"][...] = table.reshape(SHAPES["e"])
    sum_start(("e", None), 0)
    sum_middle(("o", None), 0)

    stores = []

    def store(i):
        copy = pltpu.make_async_copy(out_buf[i], outputs[i], local_out.at[i])
        copy.start()
        stores.append(copy)

    down_copy.wait()

    def finish_out(i):
        rows = rows_of(i)
        mine = pl.ds(pl.multiple_of(me * 128 + i * 32, 32), 32)
        down = r.down_part[mine, :] + r.down_other[rows, :]
        layer_out[rows, :] = (r.hidden[mine, :] + down).astype(bf16)

    loop(4, finish_out)
    store(0)
    in_copy.wait()

    def finish_in(i):
        rows = rows_of(i)
        mine = pl.ds(pl.multiple_of(me * 128 + i * 32, 32), 32)
        d_normed = r.in_part[mine, :] + r.in_other[rows, :]
        x = r.x[mine, :].astype(f32)
        inverse = inverse_rms(x)
        input_grad[rows, :] = r.d_res[mine, :] + norm_backward(d_normed, x * inverse, inverse, gain_in[...])

    loop(4, finish_in)
    store(1)

    last = {}

    def swap(name):
        last[name] = to_sibling(FIN_PAIR + SPLIT.index(name), fin[name].at[1 - me], rx[name])

    for name in ("q", "b"):
        sum_middle((name, None), 0)
    for name in MLP:
        sum_middle((name, None), 1)
    sum_end(("e", None), 0)
    sum_start(("e", None), 1)
    sum_end(("o", None), 0)
    sum_start(("o", None), 1)
    for name in MLP:
        sum_end((name, None), 1)
        sum_start((name, None), 2)
    sum_end(("e", None), 1)
    sum_start(("e", None), 2)
    for name in ("q", "b"):
        sum_end((name, None), 0)
        sum_start((name, None), 1)
    sum_end(("o", None), 1)
    sum_start(("o", None), 2)
    for name in MLP:
        sum_end((name, None), 2)
    swap("g")
    swap("u")
    store(8)
    sum_end(("e", None), 2)
    swap("e")

    def unorder(name, i, out):
        last[name].wait()
        for y in range(4):
            lanes = slice(128 * y, 128 * y + 128)
            mine, theirs = rows_at(64 * i + 8 * (2 * y + me), 8), rows_at(64 * i + 8 * (2 * y + 1 - me), 8)
            for t in range(3):
                r.blocks[mine, 128 * t : 128 * t + 128] = fin[name][me, t, :, lanes]
                r.blocks[theirs, 128 * t : 128 * t + 128] = rx[name][t, :, lanes]

    unorder("g", 0, 6)
    unorder("u", 1, 7)
    rest = r.blocks[...]
    total = jnp.zeros((128, 384), f32)
    for _ in range(3):
        head = rest.astype(bf16)
        total += dot_nt(head, r.perm[...])
        rest = rest - head.astype(f32)
    for i, out in ((0, 6), (1, 7)):
        for b in range(8):
            out_buf[out][:, 384 * b : 384 * b + 384] = total[64 * i + 8 * b : 64 * i + 8 * b + 8, :]
        store(out)
    last["e"].wait()
    out_buf[9][...] = jnp.broadcast_to(fin["e"][me] + rx["e"][...], (8, 128))
    store(9)

    for name in ("q", "b"):
        sum_end((name, None), 1)
        sum_start((name, None), 2)
    sum_end(("o", None), 2)
    store(5)
    for name in ("q", "b"):
        sum_end((name, None), 2)
        swap(name)

    def place_columns(name, out, count, width, place):
        for i in range(count):
            lanes = slice(place + i * width, place + (i + 1) * width)
            out_buf[out][:, lanes_at((2 * i + me) * width, width)] = fin[name][me, :, lanes]
            out_buf[out][:, lanes_at((2 * i + 1 - me) * width, width)] = rx[name][:, lanes]
        store(out)

    last["q"].wait()
    place_columns("q", 2, 4, 256, 0)
    last["b"].wait()
    place_columns("b", 3, 4, 128, 0)
    place_columns("b", 4, 4, 128, 512)
    for item, phase in SUMS:
        wait_for(1, item, phase, 0, 3)
    for copy in stores:
        copy.wait()


def finish_kernel(*refs):
    n = len(OUTS)
    ins, outs, held, sems = refs[:n], refs[n : 2 * n + 3], refs[2 * n + 3 : -1], refs[-1]
    fetches = [pltpu.make_async_copy(ins[i], held[i], sems.at[0, i]) for i in range(n)]
    stores = [pltpu.make_async_copy(held[i], outs[i], sems.at[1, i]) for i in range(n - 1)]
    for copy in fetches:
        copy.start()
    for fetch, copy in zip(fetches, stores):
        fetch.wait()
        copy.start()
    fetches[-1].wait()
    row = held[-1][0:1, :]
    for ref, first, count in zip(outs[n - 1 :], (0, 8, 16, 17), (8, 8, 1, 1)):
        ref[...] = row[0, first : first + count]
    for copy in stores:
        copy.wait()


def body(*args):
    vmem = pl.BlockSpec(memory_space=pltpu.VMEM)
    smem = pl.BlockSpec(memory_space=pltpu.SMEM)
    hbm = pl.BlockSpec(memory_space=pl.ANY)
    outs = [jax.ShapeDtypeStruct(*entry) for entry in OUTS]
    parts = pl.pallas_call(
        layer_kernel,
        out_shape=outs,
        in_specs=[hbm, vmem, smem, hbm, hbm, hbm, smem, smem, hbm, smem, hbm, hbm, hbm, hbm],
        out_specs=[hbm] * len(OUTS),
        scratch_shapes=[pltpu.VMEM(*entry) for group in GROUPS for entry in group.values()]
        + [pltpu.SemaphoreType.DMA((len(SEMS),))]
        + [pltpu.SemaphoreType.DMA((PAIRS,))] * 2
        + [pltpu.SemaphoreType.DMA((9,)), pltpu.SemaphoreType.DMA((len(OUTS),))],
        compiler_params=pltpu.CompilerParams(
            collective_id=1, has_side_effects=True, vmem_limit_bytes=60 << 20
        ),
        name="layer",
    )(*args)
    flat = [jax.ShapeDtypeStruct((size,), f32) for size in (8, 8, 1, 1)]
    (
        layer_out, input_grad, grad_q, grad_k, grad_v, grad_o, grad_g, grad_u, grad_d, norm_gain, mlp_gain, query_gain, key_gain,
    ) = pl.pallas_call(
        finish_kernel,
        out_shape=outs[:-1] + flat,
        in_specs=[hbm] * len(OUTS),
        out_specs=[hbm] * (len(OUTS) - 1) + [vmem] * 4,
        scratch_shapes=[pltpu.VMEM(*entry) for entry in OUTS] + [pltpu.SemaphoreType.DMA((2, len(OUTS)))],
        name="finish",
    )(*parts)
    return (
        layer_out, input_grad, norm_gain, grad_q, grad_k, grad_v, query_gain, key_gain, grad_o, mlp_gain, grad_g, grad_u, grad_d,
    )


def solution(mesh):
    rows = P(("dp", "fsdp"), None)
    flat = P(("dp", "fsdp"))
    return jax.shard_map(
        body,
        mesh=mesh,
        in_specs=(rows, rows, flat, rows, rows, rows, flat, flat, rows, flat, rows, rows, rows, rows),
        out_specs=(rows, rows, flat, rows, rows, rows, flat, flat, rows, flat, rows, rows, rows),
        check_vma=False,
    )
```

time: 172 us -> 144 us (0.84)
  Pallas kernels: 159 us -> 141 us
  local copies, waits for them, and re-layouts: 10.5 us -> 0 us
    pallas_call x1 -> x2, Pallas kernels: 159 us -> 141 us  [the longest x1 139 us: body(): pl.pallas_call(layer_kernel, out_shape=outs, in_specs=[hbm, vmem, smem, h...]
    unnamed x25 -> x0, local copies, waits for them, and re-layouts: 7.66 us -> none
    slice x2 -> x0, local copies, waits for them, and re-layouts: 2.81 us -> none  [the longest x1 1.48 us: body(): gains[:, 1]]
where the time goes in v3:
time: 144 us; the launch traced here: 143 us
  Pallas kernels  141 us (98%)
  between operations  1.95 us (1%)
    pallas_call x1, Pallas kernels, body(): pl.pallas_call(layer_kernel, out_shape=outs, in_specs=[hbm, vmem, smem, h...  139 us

profile of v3, /device:TPU:1, one launch (start us, length us, event | category | flops | bytes accessed | tf_op | source)
XLA Modules:
  0.0 143.3 jit_solution(593736138691916473)
XLA Ops:
  1.9 138.6 %layer.1 = (bf16[128,1024]{1,0:T(8,128)(2,1)}, f32[128,1024]{1,0:T(8,128)}, f32[8,2048]{1,0:T(8,128)}, f32[8,1024]{1,0:T(8,128)}, f32[8,1024]{1,0:T(8,128)}, /*i...) custom-call(bf16[128,1024]{1,0:T(8,128)(2,1)} %tokens.1, ...), custom_call_target="tpu_custom_call" | custom-call | tf_op jit(solution)/shard_map/layer/pallas_call | solution.py:936
  140.5 2.8 %finish.1 = (bf16[128,1024]{1,0:T(8,128)(2,1)}, f32[128,1024]{1,0:T(8,128)}, f32[8,2048]{1,0:T(8,128)}, f32[8,1024]{1,0:T(8,128)}, f32[8,1024]{1,0:T(8,128)}, /*...) custom-call(bf16[128,1024]{1,0:T(8,128)(2,1)} %get-tuple-element.36., ...), custom_call_target="tpu_custom_call" | custom-call | tf_op jit(solution)/shard_map/finish/pallas_call | solution.py:953

commit v4 on v3

--- a/solution.py
+++ b/solution.py
@@ -536,10 +536,10 @@
 
     loop(8, norm_in)
     normed, cot = r.normed, r.cot
-    for name in MLP:
-        gather_finish((name, None), 1)
     for name in ATTN:
         gather_forward((name, None), 2)
+    for name in MLP:
+        gather_finish((name, None), 1)
     for name in MLP:
         gather_start((name, 0), 2)
     for name in MLP:
@@ -729,7 +729,6 @@
         loop(2, rows)
 
     grad_of("o", attended, d_res_low)
-    sum_start(("o", None), 0)
     for name in MLP:
         sum_middle((name, 1), 0)
 
@@ -764,6 +763,7 @@
     loop(8, attend_back)
     for name in MLP:
         sum_middle((name, 2), 0)
+    sum_start(("o", None), 0)
 
     def in_back(i):
         y_pair = pl.ds(2 * i, 2)
@@ -778,12 +778,6 @@
     grad_of("b", normed, r.d_b)
     sum_start(("b", None), 0)
 
-    for t in range(3):
-        for name in MLP:
-            sum_end((name, t), 0)
-    for name in MLP:
-        sum_start((name, None), 1)
-
     def gain_back(i):
         x = r.x[rows_of(i), :].astype(f32)
         unit = x * inverse_rms(x)
@@ -795,7 +789,6 @@
         table += dot(jnp.where(owned, r.gain_sums[i : i + 1, :], 0.0).astype(bf16), r.eighths[i])
     weight["e"][...] = table.reshape(SHAPES["e"])
     sum_start(("e", None), 0)
-    sum_middle(("o", None), 0)
 
     stores = []
 
@@ -814,6 +807,9 @@
 
     loop(4, finish_out)
     store(0)
+    for t in range(3):
+        for name in MLP:
+            sum_end((name, t), 0)
     in_copy.wait()
 
     def finish_in(i):
@@ -832,31 +828,37 @@
     def swap(name):
         last[name] = to_sibling(FIN_PAIR + SPLIT.index(name), fin[name].at[1 - me], rx[name])
 
-    for name in ("q", "b"):
+    for name in ATTN:
         sum_middle((name, None), 0)
     for name in MLP:
-        sum_middle((name, None), 1)
+        sum_start((name, None), 1)
     sum_end(("e", None), 0)
     sum_start(("e", None), 1)
-    sum_end(("o", None), 0)
-    sum_start(("o", None), 1)
-    for name in MLP:
+    for name in ATTN:
+        sum_end((name, None), 0)
+        sum_start((name, None), 1)
+    for name in MLP:
+        sum_middle((name, None), 1)
+    sum_end(("e", None), 1)
+    sum_start(("e", None), 2)
+    for name in ATTN:
         sum_end((name, None), 1)
         sum_start((name, None), 2)
-    sum_end(("e", None), 1)
-    sum_start(("e", None), 2)
-    for name in ("q", "b"):
-        sum_end((name, None), 0)
-        sum_start((name, None), 1)
-    sum_end(("o", None), 1)
-    sum_start(("o", None), 2)
-    for name in MLP:
-        sum_end((name, None), 2)
-    swap("g")
-    swap("u")
-    store(8)
+    for name in MLP:
+        sum_end((name, None), 1)
+        sum_start((name, None), 2)
     sum_end(("e", None), 2)
     swap("e")
+    for name in ATTN:
+        sum_end((name, None), 2)
+        if name != "o":
+            swap(name)
+    store(5)
+    for name in MLP:
+        sum_end((name, None), 2)
+        if name != "d":
+            swap(name)
+    store(8)
 
     def unorder(name, i, out):
         last[name].wait()
@@ -867,6 +869,18 @@
                 r.blocks[mine, 128 * t : 128 * t + 128] = fin[name][me, t, :, lanes]
                 r.blocks[theirs, 128 * t : 128 * t + 128] = rx[name][t, :, lanes]
 
+    def place_columns(name, out, count, width, place):
+        for i in range(count):
+            lanes = slice(place + i * width, place + (i + 1) * width)
+            out_buf[out][:, lanes_at((2 * i + me) * width, width)] = fin[name][me, :, lanes]
+            out_buf[out][:, lanes_at((2 * i + 1 - me) * width, width)] = rx[name][:, lanes]
+        store(out)
+
+    last["q"].wait()
+    place_columns("q", 2, 4, 256, 0)
+    last["b"].wait()
+    place_columns("b", 3, 4, 128, 0)
+    place_columns("b", 4, 4, 128, 512)
     unorder("g", 0, 6)
     unorder("u", 1, 7)
     rest = r.blocks[...]
@@ -883,27 +897,6 @@
     out_buf[9][...] = jnp.broadcast_to(fin["e"][me] + rx["e"][...], (8, 128))
     store(9)
 
-    for name in ("q", "b"):
-        sum_end((name, None), 1)
-        sum_start((name, None), 2)
-    sum_end(("o", None), 2)
-    store(5)
-    for name in ("q", "b"):
-        sum_end((name, None), 2)
-        swap(name)
-
-    def place_columns(name, out, count, width, place):
-        for i in range(count):
-            lanes = slice(place + i * width, place + (i + 1) * width)
-            out_buf[out][:, lanes_at((2 * i + me) * width, width)] = fin[name][me, :, lanes]
-            out_buf[out][:, lanes_at((2 * i + 1 - me) * width, width)] = rx[name][:, lanes]
-        store(out)
-
-    last["q"].wait()
-    place_columns("q", 2, 4, 256, 0)
-    last["b"].wait()
-    place_columns("b", 3, 4, 128, 0)
-    place_columns("b", 4, 4, 128, 512)
     for item, phase in SUMS:
         wait_for(1, item, phase, 0, 3)
     for copy in stores:

time: 144 us -> 139 us (0.965)
  Pallas kernels: 141 us -> 136 us
    pallas_call x1, Pallas kernels: 139 us -> 134 us  [body(): pl.pallas_call(layer_kernel, out_shape=outs, in_specs=[hbm, vmem, smem, h...]
where the time goes in v4:
time: 139 us; the launch traced here: 138 us
  Pallas kernels  136 us (98%)
  between operations  1.95 us (1%)
    pallas_call x1, Pallas kernels, body(): pl.pallas_call(layer_kernel, out_shape=outs, in_specs=[hbm, vmem, smem, h...  134 us

profile of v4, /device:TPU:1, one launch (start us, length us, event | category | flops | bytes accessed | tf_op | source)
XLA Modules:
  0.0 138.3 jit_solution(12099758203366052829)
XLA Ops:
  1.9 133.6 %layer.1 = (bf16[128,1024]{1,0:T(8,128)(2,1)}, f32[128,1024]{1,0:T(8,128)}, f32[8,2048]{1,0:T(8,128)}, f32[8,1024]{1,0:T(8,128)}, f32[8,1024]{1,0:T(8,128)}, /*i...) custom-call(bf16[128,1024]{1,0:T(8,128)(2,1)} %tokens.1, ...), custom_call_target="tpu_custom_call" | custom-call | tf_op jit(solution)/shard_map/layer/pallas_call | solution.py:929
  135.6 2.8 %finish.1 = (bf16[128,1024]{1,0:T(8,128)(2,1)}, f32[128,1024]{1,0:T(8,128)}, f32[8,2048]{1,0:T(8,128)}, f32[8,1024]{1,0:T(8,128)}, f32[8,1024]{1,0:T(8,128)}, /*...) custom-call(bf16[128,1024]{1,0:T(8,128)(2,1)} %get-tuple-element.36., ...), custom_call_target="tpu_custom_call" | custom-call | tf_op jit(solution)/shard_map/finish/pallas_call | solution.py:946

commit v5 on v4

--- a/solution.py
+++ b/solution.py
@@ -27,6 +27,7 @@
 )
 NAMES = tuple(SHAPES)
 SPLIT = ("q", "b", "e", "g", "u")
+CROSS = ("q", "b", "g", "u")
 ATTN = ("q", "b", "o")
 MLP = ("g", "u", "d")
 ORDER = dict(q="xyz", g="xyz", b="yzx", u="yzx", o="zxy", d="zxy", e="zxy")
@@ -162,7 +163,7 @@
 
 
 def is_direct(item, phase):
-    return phase == 2 or item[0] == "e" or (phase == 1 and item[0] not in MLP)
+    return phase == 2 or item[0] == "e"
 
 
 GATHERS = tuple((item, phase) for item in ALL for phase in range(3) if item[0] not in MLP or phase < 2)
@@ -174,9 +175,11 @@
         for _use in range(2 if _direct else 3):
             SEMS[_kind, _item, _phase, _use] = len(SEMS)
 W = {name: (SHAPES[name], DTYPE[name]) for name in NAMES}
-STAGE = dict(q=((8, 1024), bf16), b=((8, 1024), bf16), e=((1, 128), f32), g=((3, 8, 512), bf16), u=((3, 8, 512), bf16))
-FIN = dict(q=((2, 8, 1024), f32), b=((2, 8, 1024), f32), e=((2, 1, 128), f32), g=((2, 3, 8, 512), f32), u=((2, 3, 8, 512), f32))
-RX = dict(q=((8, 1024), f32), b=((8, 1024), f32), e=((1, 128), f32), g=((3, 8, 512), f32), u=((3, 8, 512), f32))
+ROWS = {name: halved((name, None), merged((name, None), ORDER[name])) for name in CROSS}
+STAGE = {name: (ROWS[name], bf16) for name in CROSS}
+RX = {name: (ROWS[name], bf16) for name in CROSS}
+STAGE["e"] = RX["e"] = ((1, 128), f32)
+FIN = dict(e=((2, 1, 128), f32))
 FAR, NEAR = {}, {}
 for _item, _phase in SUMS:
     _shape = merged(_item, ORDER[_item[0]][::-1][: _phase + 1])
@@ -189,13 +192,13 @@
 INS = (
     ((8, 2048), f32), ((8, 1024), f32), ((8, 1024), f32), ((16, 1024), f32), ((8, 3072), f32), ((8, 3072), f32), ((24, 1024), f32),
 )
-OUTS = (((128, 1024), bf16), ((128, 1024), f32)) + INS + (((8, 128), f32),)
+OUTS = (((128, 1024), bf16), ((128, 1024), f32)) + INS + tuple(((size,), f32) for size in (8, 8, 1, 1))
 IN_BUF = {i: entry for i, entry in enumerate(INS)}
-OUT_BUF = {i: entry for i, entry in enumerate(OUTS)}
 FLAT = dict(
     x=((256, 1024), bf16),
     cot=((256, 1024), bf16),
     seg=((2, 8, 128), jnp.int32),
+    seg_in=((1, 128), jnp.int32),
     perm=((384, 384), bf16),
     blocks=((128, 384), f32),
     eighths=((2, 1024, 128), bf16),
@@ -233,7 +236,7 @@
     in_part=((256, 1024), f32),
     in_other=((128, 1024), f32),
 )
-GROUPS = (W, STAGE, FIN, RX, FAR, NEAR, IN_BUF, OUT_BUF, FLAT)
+GROUPS = (W, STAGE, FIN, RX, FAR, NEAR, IN_BUF, FLAT)
 X_PAIR, COT_PAIR, SEG_PAIR, OUT_PAIR, DOWN_PAIR, MID_PAIR, IN_PAIR, STAGE_PAIR = range(8)
 FIN_PAIR = STAGE_PAIR + len(SPLIT)
 PAIRS = FIN_PAIR + len(SPLIT)
@@ -244,16 +247,17 @@
     cotangent, *refs,
 ):
     refs = list(refs)
-    outputs = [refs.pop(0) for _ in OUTS]
+    out_buf = [refs.pop(0) for _ in OUTS]
     held = []
     for group in GROUPS:
         held.append({key: refs.pop(0) for key in group})
-    weight, stage, fin, rx, far_of, near_of, in_buf, out_buf, flat = held
+    weight, stage, fin, rx, far_of, near_of, in_buf, flat = held
     r = types.SimpleNamespace(**flat)
-    sems, pair_send, pair_recv, local_in, local_out = refs
+    gains_in, (sems, pair_send, pair_recv, local_in) = refs[:4], refs[4:]
     pos = coords()
     me = pos["c"]
     sibling = device(pos, "c")
+    flipped = dict(pos, c=1 - me)
     own_rows = pl.ds(pl.multiple_of(me * 128, 128), 128)
     other_rows = pl.ds(pl.multiple_of((1 - me) * 128, 128), 128)
     layer_out, input_grad = out_buf[0], out_buf[1]
@@ -262,6 +266,8 @@
     others = [sibling]
     for axis in "xyz":
         others += [device(pos, axis, step) for step in (1, -1, 2)]
+    for axis in "xy":
+        others += [device(flipped, axis, step) for step in (1, -1, 2)]
     for other in others:
         pl.semaphore_signal(barrier, inc=1, device_id=other, device_id_type=MESH)
     fetches = []
@@ -269,8 +275,12 @@
         fetches.append(pltpu.make_async_copy(src, in_buf[i], local_in.at[i]))
     fetches.append(pltpu.make_async_copy(tokens, r.x.at[own_rows], local_in.at[7]))
     fetches.append(pltpu.make_async_copy(cotangent, r.cot.at[own_rows], local_in.at[8]))
-    for copy in fetches:
+    small = ((norm_gain, gains_in[0]), (mlp_gain, gains_in[1]), (query_gain, gains_in[2]), (key_gain, gains_in[3]), (segment, r.seg_in))
+    for i, (src, dst) in enumerate(small):
+        fetches.append(pltpu.make_async_copy(src, dst, local_in.at[9 + i]))
+    for copy in fetches[9:] + fetches[:9]:
         copy.start()
+    norm_gain, mlp_gain, query_gain, key_gain = gains_in
 
     def remote(src, dst, send_sem, recv_sem, target):
         return pltpu.make_async_remote_copy(
@@ -298,10 +308,18 @@
         name, third = item
         return weight[name] if third is None else weight[name].at[third]
 
+    pairs = {}
+
     def gather_start(item, phase, keys=(0, 1, 2, 3)):
         order = ORDER[item[0]]
         axis = order[phase]
         at = {a: pos[a] for a in order[phase:]}
+        if phase == 0 and item[0] in CROSS:
+            mine = block(view(item), item, at, me)
+            for step in (1, -1, 2):
+                send(0, item, phase, 1, mine, mine, device(pos, axis, step))
+                send(0, item, phase, 1, stage[item[0]], mine, device(flipped, axis, step))
+            return
         if phase == 0 or item[0] == "e":
             for step in (1, -1, 2):
                 src = block(view(item), item, at)
@@ -340,7 +358,15 @@
         def part(place, half=None):
             return block(cur, item, {**at, axis: place}, half)
 
-        if is_direct(item, phase):
+        if phase == 2 and item[0] in CROSS:
+            ways = ((opposite, far_of[item, phase, 2], 2), (ahead, near_up, 1), (behind, near_down, -1))
+            for place, dst, step in ways:
+                slot = half_of(dst, item, me)
+                send(1, item, phase, 1, part(place, me), slot, device(pos, axis, step))
+                send(1, item, phase, 1, part(place, 1 - me), slot, device(flipped, axis, step))
+            index = FIN_PAIR + SPLIT.index(item[0])
+            pairs[index] = to_sibling(index, block(cur, item, pos, 1 - me), rx[item[0]])
+        elif is_direct(item, phase):
             send(1, item, phase, 1, part(opposite), far_of[item, phase, 2], across)
             send(1, item, phase, 1, part(ahead), near_up, up)
             send(1, item, phase, 1, part(behind), near_down, down)
@@ -375,26 +401,47 @@
             add_into(sources[0], sources, merged(item, order[: phase + 1]))
             return
 
-        def total(place):
-            value = sources[0][place].astype(f32)
+        name = item[0]
+
+        def total(place, first=None):
+            value = (sources[0] if first is None else first)[place].astype(f32)
             for source in sources[1:]:
                 value = value + source[place].astype(f32)
             return value
 
-        name = item[0]
-        if name in MLP:
+        def both(t):
+            lead = () if t is None else (t,)
+            mine = total(lead + (0, me, 0, 0))
+            theirs = rx[name][lead + (0, 0, 0, 0)].astype(f32)
+            for source in sources[1:]:
+                theirs = theirs + source[lead + (0, 1 - me, 0, 0)].astype(f32)
+            return mine, theirs
+
+        if name in CROSS:
+            pairs[FIN_PAIR + SPLIT.index(name)].wait()
+        if name == "d":
             for t in range(3):
-                if name == "d":
-                    out_buf[8][8 * t : 8 * t + 8, :] = total((t, 0, 0, 0))
-                else:
-                    for c in range(2):
-                        fin[name][c, t] = total((t, 0, c, 0, 0))
+                out_buf[8][8 * t : 8 * t + 8, :] = total((t, 0, 0, 0))
         elif name == "o":
             for t in range(2):
                 out_buf[5][8 * t : 8 * t + 8, :] = total((0, 0, 0, t))
+        elif name == "e":
+            for c in range(2):
+                fin["e"][c] = total((0, c, 0, 0))
+        elif name in MLP:
+            start = 0 if name == "g" else 64
+            for t in range(3):
+                columns = slice(128 * t, 128 * t + 128)
+                for core, value in zip((me, 1 - me), both(t)):
+                    for y in range(4):
+                        r.blocks[rows_at(start + 8 * (2 * y + core), 8), columns] = value[:, 128 * y : 128 * y + 128]
         else:
-            for c in range(2):
-                fin[name][c] = total((0, c, 0, 0))
+            layouts = ((2, 4, 256, 0),) if name == "q" else ((3, 4, 128, 0), (4, 4, 128, 512))
+            for core, value in zip((me, 1 - me), both(None)):
+                for out, count, width, place in layouts:
+                    for i in range(count):
+                        lanes = slice(place + i * width, place + (i + 1) * width)
+                        out_buf[out][:, lanes_at((2 * i + core) * width, width)] = value[:, lanes]
 
     spot = (pos["y"], me, pos["z"], pos["x"])
 
@@ -402,11 +449,14 @@
         for i in range(count):
             lanes = slice(place + i * width, place + (i + 1) * width)
             weight[name][spot + (slice(None), lanes)] = in_buf[buf][:, lanes_at((2 * i + me) * width, width)].astype(bf16)
-            stage[name][:, lanes] = in_buf[buf][:, lanes_at((2 * i + 1 - me) * width, width)].astype(bf16)
+            theirs = in_buf[buf][:, lanes_at((2 * i + 1 - me) * width, width)].astype(bf16)
+            stage[name][0, 0, 0, 0, :, lanes] = theirs
 
     row_id = lax.broadcasted_iota(jnp.int32, (8, 128), 0)
     lane_id = lax.broadcasted_iota(jnp.int32, (8, 128), 1)
     lane_row = lax.broadcasted_iota(jnp.int32, (1, 128), 1)
+    for copy in fetches[9:]:
+        copy.wait()
     gains = jnp.zeros((1, 128), f32)
     for i in range(8):
         gains = jnp.where(lane_row == i, norm_gain[i], gains)
@@ -415,7 +465,7 @@
     gains = jnp.where(lane_row == 17, key_gain[0], gains).astype(bf16).astype(f32)
     weight["e"][spot] = gains
     stage["e"][...] = gains
-    r.seg[me] = jnp.broadcast_to(segment[...], (8, 128))
+    r.seg[me] = jnp.broadcast_to(r.seg_in[...], (8, 128))
     for i in range(4):
         fetches[i].wait()
     stage_columns("q", 0, 0, 4, 256, 0)
@@ -425,17 +475,16 @@
         weight["o"][pos["y"], pos["z"], pos["x"], t] = in_buf[3][8 * t : 8 * t + 8, :].astype(bf16)
 
     pl.semaphore_wait(barrier, len(others))
-    pairs = {}
 
     def pair_start(name):
         index = STAGE_PAIR + SPLIT.index(name)
-        if name in MLP:
-            dst = weight[name].at[:, pos["y"], me, pos["z"], pos["x"]]
-        else:
-            dst = weight[name].at[spot]
+        dst = weight["e"].at[spot] if name == "e" else block(weight[name], (name, None), pos, me)
         pairs[name] = to_sibling(index, stage[name], dst)
 
-    for name in ("q", "b", "e"):
+    pair_start("e")
+    for name in ATTN:
+        gather_start((name, None), 0)
+    for name in ("q", "b"):
         pair_start(name)
 
     to_lane = lax.broadcasted_iota(jnp.int32, (384, 384), 1)
@@ -454,28 +503,28 @@
             for t in range(3):
                 lanes = slice(128 * y, 128 * y + 128)
                 weight[name][(t,) + spot + (slice(None), lanes)] = mine[:, 128 * t : 128 * t + 128]
-                stage[name][t, :, lanes] = theirs[:, 128 * t : 128 * t + 128]
+                stage[name][t, 0, 0, 0, 0, :, lanes] = theirs[:, 128 * t : 128 * t + 128]
     for t in range(3):
         weight["d"][t, pos["y"], pos["z"], pos["x"]] = in_buf[6][8 * t : 8 * t + 8, :].astype(bf16)
+    pairs["e"].wait()
+    gather_start(("e", None), 0)
+    for name in MLP:
+        gather_start((name, None), 0)
     for name in ("g", "u"):
         pair_start(name)
-    for name in ("e", "q", "b"):
-        pairs[name].wait()
-    for name in ("e", "q", "b", "o"):
-        gather_start((name, None), 0)
-    for name in ("g", "u"):
-        pairs[name].wait()
-    for name in MLP:
-        gather_start((name, None), 0)
     fetches[7].wait()
     fetches[8].wait()
     pairs[X_PAIR] = to_sibling(X_PAIR, r.x.at[own_rows], r.x.at[own_rows])
     pairs[SEG_PAIR] = to_sibling(SEG_PAIR, r.seg.at[me], r.seg.at[me])
     pairs[COT_PAIR] = to_sibling(COT_PAIR, r.cot.at[own_rows], r.cot.at[own_rows])
     for name in ("e",) + ATTN:
+        if name in CROSS:
+            pairs[name].wait()
         gather_finish((name, None), 0)
         gather_start((name, None), 1)
     for name in MLP:
+        if name in CROSS:
+            pairs[name].wait()
         gather_finish((name, None), 0)
         gather_start((name, None), 1, (0, 1))
 
@@ -790,13 +839,6 @@
     weight["e"][...] = table.reshape(SHAPES["e"])
     sum_start(("e", None), 0)
 
-    stores = []
-
-    def store(i):
-        copy = pltpu.make_async_copy(out_buf[i], outputs[i], local_out.at[i])
-        copy.start()
-        stores.append(copy)
-
     down_copy.wait()
 
     def finish_out(i):
@@ -806,7 +848,6 @@
         layer_out[rows, :] = (r.hidden[mine, :] + down).astype(bf16)
 
     loop(4, finish_out)
-    store(0)
     for t in range(3):
         for name in MLP:
             sum_end((name, t), 0)
@@ -821,12 +862,6 @@
         input_grad[rows, :] = r.d_res[mine, :] + norm_backward(d_normed, x * inverse, inverse, gain_in[...])
 
     loop(4, finish_in)
-    store(1)
-
-    last = {}
-
-    def swap(name):
-        last[name] = to_sibling(FIN_PAIR + SPLIT.index(name), fin[name].at[1 - me], rx[name])
 
     for name in ATTN:
         sum_middle((name, None), 0)
@@ -842,47 +877,17 @@
     sum_end(("e", None), 1)
     sum_start(("e", None), 2)
     for name in ATTN:
+        sum_middle((name, None), 1)
+    for name in MLP:
         sum_end((name, None), 1)
         sum_start((name, None), 2)
-    for name in MLP:
+    for name in ATTN:
         sum_end((name, None), 1)
         sum_start((name, None), 2)
     sum_end(("e", None), 2)
-    swap("e")
-    for name in ATTN:
+    swap = to_sibling(FIN_PAIR + SPLIT.index("e"), fin["e"].at[1 - me], rx["e"])
+    for name in MLP:
         sum_end((name, None), 2)
-        if name != "o":
-            swap(name)
-    store(5)
-    for name in MLP:
-        sum_end((name, None), 2)
-        if name != "d":
-            swap(name)
-    store(8)
-
-    def unorder(name, i, out):
-        last[name].wait()
-        for y in range(4):
-            lanes = slice(128 * y, 128 * y + 128)
-            mine, theirs = rows_at(64 * i + 8 * (2 * y + me), 8), rows_at(64 * i + 8 * (2 * y + 1 - me), 8)
-            for t in range(3):
-                r.blocks[mine, 128 * t : 128 * t + 128] = fin[name][me, t, :, lanes]
-                r.blocks[theirs, 128 * t : 128 * t + 128] = rx[name][t, :, lanes]
-
-    def place_columns(name, out, count, width, place):
-        for i in range(count):
-            lanes = slice(place + i * width, place + (i + 1) * width)
-            out_buf[out][:, lanes_at((2 * i + me) * width, width)] = fin[name][me, :, lanes]
-            out_buf[out][:, lanes_at((2 * i + 1 - me) * width, width)] = rx[name][:, lanes]
-        store(out)
-
-    last["q"].wait()
-    place_columns("q", 2, 4, 256, 0)
-    last["b"].wait()
-    place_columns("b", 3, 4, 128, 0)
-    place_columns("b", 4, 4, 128, 512)
-    unorder("g", 0, 6)
-    unorder("u", 1, 7)
     rest = r.blocks[...]
     total = jnp.zeros((128, 384), f32)
     for _ in range(3):
@@ -892,63 +897,53 @@
     for i, out in ((0, 6), (1, 7)):
         for b in range(8):
             out_buf[out][:, 384 * b : 384 * b + 384] = total[64 * i + 8 * b : 64 * i + 8 * b + 8, :]
-        store(out)
-    last["e"].wait()
-    out_buf[9][...] = jnp.broadcast_to(fin["e"][me] + rx["e"][...], (8, 128))
-    store(9)
-
+    swap.wait()
+    row = fin["e"][me] + rx["e"][...]
+    for ref, first, count in zip(out_buf[9:], (0, 8, 16, 17), (8, 8, 1, 1)):
+        ref[...] = row[0, first : first + count]
+    for name in ATTN:
+        sum_end((name, None), 2)
     for item, phase in SUMS:
         wait_for(1, item, phase, 0, 3)
-    for copy in stores:
-        copy.wait()
 
 
 def finish_kernel(*refs):
     n = len(OUTS)
-    ins, outs, held, sems = refs[:n], refs[n : 2 * n + 3], refs[2 * n + 3 : -1], refs[-1]
-    fetches = [pltpu.make_async_copy(ins[i], held[i], sems.at[0, i]) for i in range(n)]
-    stores = [pltpu.make_async_copy(held[i], outs[i], sems.at[1, i]) for i in range(n - 1)]
-    for copy in fetches:
+    ins, outs, sems = refs[:n], refs[n : 2 * n], refs[-1]
+    copies = [pltpu.make_async_copy(ins[i], outs[i], sems.at[i]) for i in range(n)]
+    for copy in copies:
         copy.start()
-    for fetch, copy in zip(fetches, stores):
-        fetch.wait()
-        copy.start()
-    fetches[-1].wait()
-    row = held[-1][0:1, :]
-    for ref, first, count in zip(outs[n - 1 :], (0, 8, 16, 17), (8, 8, 1, 1)):
-        ref[...] = row[0, first : first + count]
-    for copy in stores:
+    for copy in copies:
         copy.wait()
 
 
 def body(*args):
+    hbm = pl.BlockSpec(memory_space=pl.ANY)
     vmem = pl.BlockSpec(memory_space=pltpu.VMEM)
-    smem = pl.BlockSpec(memory_space=pltpu.SMEM)
-    hbm = pl.BlockSpec(memory_space=pl.ANY)
-    outs = [jax.ShapeDtypeStruct(*entry) for entry in OUTS]
     parts = pl.pallas_call(
         layer_kernel,
-        out_shape=outs,
-        in_specs=[hbm, vmem, smem, hbm, hbm, hbm, smem, smem, hbm, smem, hbm, hbm, hbm, hbm],
-        out_specs=[hbm] * len(OUTS),
+        out_shape=[pltpu.VMEM(*entry) for entry in OUTS],
+        in_specs=[hbm] * 14,
+        out_specs=[vmem] * len(OUTS),
         scratch_shapes=[pltpu.VMEM(*entry) for group in GROUPS for entry in group.values()]
+        + [pltpu.SMEM((size,), f32) for size in (8, 8, 1, 1)]
         + [pltpu.SemaphoreType.DMA((len(SEMS),))]
         + [pltpu.SemaphoreType.DMA((PAIRS,))] * 2
-        + [pltpu.SemaphoreType.DMA((9,)), pltpu.SemaphoreType.DMA((len(OUTS),))],
+        + [pltpu.SemaphoreType.DMA((14,))],
         compiler_params=pltpu.CompilerParams(
-            collective_id=1, has_side_effects=True, vmem_limit_bytes=60 << 20
+            collective_id=1, has_side_effects=True, vmem_limit_bytes=57 << 20
         ),
         name="layer",
     )(*args)
-    flat = [jax.ShapeDtypeStruct((size,), f32) for size in (8, 8, 1, 1)]
+    parts = [pltpu.with_memory_space_constraint(part, pltpu.VMEM) for part in parts]
     (
         layer_out, input_grad, grad_q, grad_k, grad_v, grad_o, grad_g, grad_u, grad_d, norm_gain, mlp_gain, query_gain, key_gain,
     ) = pl.pallas_call(
         finish_kernel,
-        out_shape=outs[:-1] + flat,
-        in_specs=[hbm] * len(OUTS),
-        out_specs=[hbm] * (len(OUTS) - 1) + [vmem] * 4,
-        scratch_shapes=[pltpu.VMEM(*entry) for entry in OUTS] + [pltpu.SemaphoreType.DMA((2, len(OUTS)))],
+        out_shape=[jax.ShapeDtypeStruct(*entry) for entry in OUTS],
+        in_specs=[vmem] * len(OUTS),
+        out_specs=[hbm] * len(OUTS),
+        scratch_shapes=[pltpu.SemaphoreType.DMA((len(OUTS),))],
         name="finish",
     )(*parts)
     return (

time: 139 us -> 133 us (0.957)
  Pallas kernels: 136 us -> 131 us
    pallas_call x2, Pallas kernels: 136 us -> 131 us  [the longest x1 129 us: body(): pl.pallas_call(layer_kernel, out_shape=[pltpu.VMEM(*entry) for entry in O...]
where the time goes in v5:
time: 133 us
  Pallas kernels  131 us (98%)
  between operations  2.11 us (2%)
    pallas_call x1, Pallas kernels, body(): pl.pallas_call(layer_kernel, out_shape=[pltpu.VMEM(*entry) for entry in O...  129 us

profile of v5, /device:TPU:1, one launch (start us, length us, event | category | flops | bytes accessed | tf_op | source)
XLA Modules:
  0.0 133.3 jit_solution(4091914527930528264)
XLA Ops:
  1.9 128.8 %layer.1 = (bf16[128,1024]{1,0:T(8,128)(2,1)S(1)}, f32[128,1024]{1,0:T(8,128)S(1)}, f32[8,2048]{1,0:T(8,128)S(1)}, f32[8,1024]{1,0:T(8,128)S(1)}, f32[8,1024]{1,...) custom-call(bf16[128,1024]{1,0:T(8,128)(2,1)} %tokens.1, ...), custom_call_target="tpu_custom_call" | custom-call | tf_op jit(solution)/shard_map/layer/pallas_call | solution.py:923
  130.8 2.4 %finish.1 = (bf16[128,1024]{1,0:T(8,128)(2,1)}, f32[128,1024]{1,0:T(8,128)}, f32[8,2048]{1,0:T(8,128)}, f32[8,1024]{1,0:T(8,128)}, f32[8,1024]{1,0:T(8,128)}, /*...) custom-call(bf16[128,1024]{1,0:T(8,128)(2,1)S(1)} %get-tuple-element, ...), custom_call_target="tpu_custom_call" | custom-call | tf_op jit(solution)/shard_map/finish/pallas_call | solution.py:941

commit v6 on v5

--- a/solution.py
+++ b/solution.py
@@ -171,6 +171,8 @@
 SEMS = {}
 for _kind, _steps in enumerate((GATHERS, SUMS)):
     for _item, _phase in _steps:
+        if _item[0] in ("u", "d"):
+            continue
         _direct = is_direct(_item, _phase) if _kind else _phase == 0 or _item[0] == "e"
         for _use in range(2 if _direct else 3):
             SEMS[_kind, _item, _phase, _use] = len(SEMS)
@@ -293,15 +295,22 @@
         return copy
 
     def sem(kind, item, phase, use):
-        return sems.at[SEMS[kind, item, phase, use]]
+        name, third = item
+        return sems.at[SEMS[kind, ("g" if name in MLP else name, third), phase, use]]
 
     def send(kind, item, phase, use, src, dst, target):
         remote(src, dst, sem(kind, item, phase, 0), sem(kind, item, phase, use), target).start()
 
     def wait_for(kind, item, phase, use, count):
-        order = ORDER[item[0]] if kind == 0 else ORDER[item[0]][::-1]
+        name, third = item
+        if name in ("u", "d"):
+            return
+        order = ORDER[name] if kind == 0 else ORDER[name][::-1]
         fixed = order[phase + 1 :] if kind == 0 else order[:phase]
-        like = block(view(item), item, {**{a: pos[a] for a in fixed}, order[phase]: (0, count)})
+        at = {a: pos[a] for a in fixed}
+        if name == "g" and third is None:
+            at[fixed[0]] = (0, 3)
+        like = block(weight[name], (name, None), {**at, order[phase]: (0, count)})
         pltpu.make_async_copy(like, like, sem(kind, item, phase, use)).wait()
 
     def view(item):

time: 133 us -> 133 us (level)
  no operation moved by 1% of the time
where the time goes in v6:
time: 133 us
  Pallas kernels  131 us (98%)
  between operations  2.11 us (2%)
    pallas_call x1, Pallas kernels, body(): pl.pallas_call(layer_kernel, out_shape=[pltpu.VMEM(*entry) for entry in O...  128 us

profile of v6, /device:TPU:1, one launch (start us, length us, event | category | flops | bytes accessed | tf_op | source)
XLA Modules:
  0.0 132.8 jit_solution(1230388465715233835)
XLA Ops:
  1.9 128.3 %layer.1 = (bf16[128,1024]{1,0:T(8,128)(2,1)S(1)}, f32[128,1024]{1,0:T(8,128)S(1)}, f32[8,2048]{1,0:T(8,128)S(1)}, f32[8,1024]{1,0:T(8,128)S(1)}, f32[8,1024]{1,...) custom-call(bf16[128,1024]{1,0:T(8,128)(2,1)} %tokens.1, ...), custom_call_target="tpu_custom_call" | custom-call | tf_op jit(solution)/shard_map/layer/pallas_call | solution.py:932
  130.2 2.4 %finish.1 = (bf16[128,1024]{1,0:T(8,128)(2,1)}, f32[128,1024]{1,0:T(8,128)}, f32[8,2048]{1,0:T(8,128)}, f32[8,1024]{1,0:T(8,128)}, f32[8,1024]{1,0:T(8,128)}, /*...) custom-call(bf16[128,1024]{1,0:T(8,128)(2,1)S(1)} %get-tuple-element, ...), custom_call_target="tpu_custom_call" | custom-call | tf_op jit(solution)/shard_map/finish/pallas_call | solution.py:950

commit v7 on v6

--- a/solution.py
+++ b/solution.py
@@ -709,13 +709,19 @@
             got = dot_tn(mixed[:, lanes_at(i * 256, 256)], cot[...]).astype(bf16)
             weight["d"][t, pl.ds(2 * i, 2)] = got.reshape(2, 4, 4, 8, 1024)
 
-        def grad_gate(i):
-            left = mid_low[:, lanes_at(i * 512, 512)]
-            weight["g"][t, pl.ds(2 * i, 2)] = dot_tn(left, d_gate[...]).astype(bf16).reshape(2, 2, 4, 4, 8, 512)
-            weight["u"][t, pl.ds(2 * i, 2)] = dot_tn(left, d_up[...]).astype(bf16).reshape(2, 2, 4, 4, 8, 512)
+        def grad_columns(name, right):
+            def rows(i):
+                left = mid_low[:, lanes_at(i * 512, 512)]
+                weight[name][t, pl.ds(2 * i, 2)] = dot_tn(left, right[...]).astype(bf16).reshape(2, 2, 4, 4, 8, 512)
+
+            return rows
 
         loop(2, grad_down)
-        loop(2, grad_gate)
+        sum_start(("d", t), 0)
+        loop(2, grad_columns("g", d_gate))
+        sum_start(("g", t), 0)
+        loop(2, grad_columns("u", d_up))
+        sum_start(("u", t), 0)
 
     def sends_done(item, phases):
         for phase in phases:
@@ -731,23 +737,17 @@
         sends_done((name, 0), (2,))
     grads(0)
     for name in MLP:
-        sum_start((name, 0), 0)
-    for name in MLP:
         gather_finish((name, 1), 2)
     feed(1)
     for name in MLP:
         sends_done((name, 1), (2,))
     grads(1)
     for name in MLP:
-        sum_start((name, 1), 0)
-    for name in MLP:
         gather_finish((name, 2), 2)
     feed(2)
     for name in MLP:
         sends_done((name, 2), (2,))
     grads(2)
-    for name in MLP:
-        sum_start((name, 2), 0)
     down_copy = to_sibling(DOWN_PAIR, r.down_part.at[other_rows], r.down_other)
     for name in MLP:
         sum_middle((name, 0), 0)

time: 133 us -> 133 us (level)
  no operation moved by 1% of the time
where the time goes in v7:
time: 133 us
  Pallas kernels  131 us (98%)
  between operations  2.11 us (2%)
    pallas_call x1, Pallas kernels, body(): pl.pallas_call(layer_kernel, out_shape=[pltpu.VMEM(*entry) for entry in O...  128 us

profile of v7, /device:TPU:1, one launch (start us, length us, event | category | flops | bytes accessed | tf_op | source)
XLA Modules:
  0.0 132.8 jit_solution(7049415927148236678)
XLA Ops:
  1.9 128.3 %layer.1 = (bf16[128,1024]{1,0:T(8,128)(2,1)S(1)}, f32[128,1024]{1,0:T(8,128)S(1)}, f32[8,2048]{1,0:T(8,128)S(1)}, f32[8,1024]{1,0:T(8,128)S(1)}, f32[8,1024]{1,...) custom-call(bf16[128,1024]{1,0:T(8,128)(2,1)} %tokens.1, ...), custom_call_target="tpu_custom_call" | custom-call | tf_op jit(solution)/shard_map/layer/pallas_call | solution.py:932
  130.2 2.4 %finish.1 = (bf16[128,1024]{1,0:T(8,128)(2,1)}, f32[128,1024]{1,0:T(8,128)}, f32[8,2048]{1,0:T(8,128)}, f32[8,1024]{1,0:T(8,128)}, f32[8,1024]{1,0:T(8,128)}, /*...) custom-call(bf16[128,1024]{1,0:T(8,128)(2,1)S(1)} %get-tuple-element, ...), custom_call_target="tpu_custom_call" | custom-call | tf_op jit(solution)/shard_map/finish/pallas_call | solution.py:950
